TPU v7x, 32 devices: a whole 2x2x4 slice. The times are simulated.
32 devices in a mesh: dp: 8 (over z, x), row: 2 (over core), col: 2 (over y).
Axes of the slice: x: 2, y: 2, z: 4, core: 2. Of those that a mesh axis runs over, the one named last changes fastest.
Arguments:
- tokens_in: bfloat16 [16384, 768], P(('dp', 'row'), 'col'), may hold values from -6 to 6
- teacher: bfloat16 [16384, 768], P(('dp', 'row'), 'col'), may hold values from -6 to 6
- qkv_weight: bfloat16 [2, 768, 3, 768], P(None, 'col', None, 'row'), may hold values from -0.21875 to 0.21875
- query_bias: float32 [2, 768], P(None, 'row'), may hold values from -3 to 3
- out_weight: bfloat16 [2, 768, 768], P(None, 'row', 'col'), may hold values from -2.5 to 2.5
- out_bias: float32 [2, 768], P(None, 'col'), may hold values from -3 to 3
- first_gain: float32 [2, 768], P(None, 'col'), may hold values from 0.25 to 1.75
- first_shift: float32 [2, 768], P(None, 'col'), may hold values from -3 to 3
- up_weight: bfloat16 [2, 768, 3072], P(None, 'col', 'row'), may hold values from -0.21875 to 0.21875
- up_bias: float32 [2, 3072], P(None, 'row'), may hold values from -3 to 3
- down_weight: bfloat16 [2, 3072, 768], P(None, 'row', 'col'), may hold values from -0.109375 to 0.109375
- down_bias: float32 [2, 768], P(None, 'col'), may hold values from -3 to 3
- second_gain: float32 [2, 768], P(None, 'col'), may hold values from 0.25 to 1.75
- second_shift: float32 [2, 768], P(None, 'col'), may hold values from -3 to 3
- random_blocks: int32 [2, 12, 14, 3], replicated, may hold values from 0 to 15
- segment_ids: int32 [16, 1024], P('dp'), may hold values from 0 to 3, never falling along the last dimension, each value on 1 to 512 neighbouring positions
- padding_mask: int32 [16, 1024], P('dp'), may hold values from 0 to 1, as said below
Outputs:
- hidden_out: float32 [16384, 768], P(('dp', 'row'), 'col')
- loss: float32 [], replicated
- input_grad: float32 [16384, 768], P(('dp', 'row'), 'col')
- grad_query_key_weight: float32 [2, 768, 2, 768], P(None, 'col', None, 'row')
- grad_value_weight: float32 [2, 768, 768], P(None, 'col', 'row')
- grad_query_bias: float32 [2, 768], P(None, 'row')
- grad_out_weight: float32 [2, 768, 768], P(None, 'row', 'col')
- grad_out_bias: float32 [2, 768], P(None, 'col')
- grad_first_gain: float32 [2, 768], P(None, 'col')
- grad_first_shift: float32 [2, 768], P(None, 'col')
- grad_up_weight: float32 [2, 768, 3072], P(None, 'col', 'row')
- grad_up_bias: float32 [2, 3072], P(None, 'row')
- grad_down_weight: float32 [2, 3072, 768], P(None, 'row', 'col')
- grad_down_bias: float32 [2, 768], P(None, 'col')
- grad_second_gain: float32 [2, 768], P(None, 'col')
- grad_second_shift: float32 [2, 768], P(None, 'col')
Inputs may be any that keep to these rules, and one draw needn't show every extreme that they name: `padding_mask`: 1 marks a real token; the real tokens of each sequence form its prefix, one token long at least.
All inputs are finite; a program needn't handle non-finite values.
Results may differ from a plain program's by a relative error of at most 0.03.
Values may be sent and summed in bfloat16 or wider, within the bound.
No kernel may reach another device: no remote copies, remote signals or barrier semaphores. Data moves between devices by JAX's collectives and lax.ppermute only.
A program may use at most 256 MiB of HBM per device.

v0:
```python
from functools import partial

import jax
import jax.numpy as jnp
from jax import lax
from jax.sharding import PartitionSpec as P

BLK = 64


EPSILON = 1e-06
MASKED_SCORE = -1e30


def block_lists(random_blocks):
    count = random_blocks.shape[-2] + 2
    index = jnp.arange(1, count - 1, dtype=jnp.int32)
    window = jnp.stack(
        [jnp.zeros_like(index), jnp.full_like(index, count - 1), index - 1, index, index + 1],
        axis=1,
    )
    window = jnp.broadcast_to(window, random_blocks.shape[:-1] + (5,))
    listed = jnp.concatenate([window, random_blocks], axis=-1)
    total = listed.shape[-1]
    earlier = jnp.arange(total)[:, None] > jnp.arange(total)[None, :]
    repeated = jnp.any((listed[..., :, None] == listed[..., None, :]) & earlier, axis=-1)
    return (listed, jnp.logical_not(repeated))


def allowed_pairs(query_pos, key_pos, segment, valid):
    same = segment[query_pos][..., :, None] == segment[key_pos][..., None, :]
    live = (valid[query_pos] > 0)[..., :, None] & (valid[key_pos] > 0)[..., None, :]
    itself = query_pos[..., :, None] == key_pos[..., None, :]
    return same & live | itself


def sequence_masks(segment, valid, listed, kept, blk):
    length = segment.shape[0]
    heads_count, middle = (listed.shape[0], listed.shape[1])
    position = jnp.arange(length, dtype=jnp.int32)
    edge_pos = jnp.concatenate([position[:blk], position[length - blk :]])
    edge_mask = allowed_pairs(edge_pos, position, segment, valid)
    mid_pos = jnp.broadcast_to(
        position[blk : length - blk].reshape(1, middle, blk), (heads_count, middle, blk)
    )
    key_pos = (listed[..., None] * blk + jnp.arange(blk, dtype=jnp.int32)).reshape(
        heads_count, middle, -1
    )
    mid_mask = (
        allowed_pairs(mid_pos, key_pos, segment, valid)
        & jnp.repeat(kept, blk, axis=-1)[..., None, :]
    )
    return (edge_mask, mid_mask)


def block_chooser(listed, count, dtype):
    return (listed[..., None] == jnp.arange(count, dtype=jnp.int32)).astype(dtype)


def near_blocks(table, listed, blk):
    heads_count, length, width = table.shape
    blocks = table.reshape(heads_count, length // blk, blk, width)
    chooser = block_chooser(listed, length // blk, table.dtype)
    picked = jnp.einsum("hmjb,hbtw->hmjtw", chooser, blocks, preferred_element_type=table.dtype)
    return picked.reshape(heads_count, listed.shape[1], -1, width)


def spread_blocks(near, listed, blk, length):
    heads_count, middle, width = (near.shape[0], near.shape[1], near.shape[-1])
    pieces = near.reshape(heads_count, middle, listed.shape[2], blk, width)
    chooser = block_chooser(listed, length // blk, jnp.float32)
    summed = jnp.einsum("hmjb,hmjtw->hbtw", chooser, pieces, precision=lax.Precision.HIGHEST)
    return summed.reshape(heads_count, length, width)


def edge_rows(table, blk):
    return jnp.concatenate([table[:, :blk], table[:, table.shape[1] - blk :]], axis=1)


def middle_rows(table, blk):
    heads_count, length, width = table.shape
    return table[:, blk : length - blk].reshape(heads_count, length // blk - 2, blk, width)


def softmax_parts(scores, mask):
    masked = jnp.where(mask, scores, MASKED_SCORE)
    top = jnp.max(masked, axis=-1, keepdims=True)
    weights = jnp.exp(masked - top)
    total = jnp.sum(weights, axis=-1, keepdims=True)
    return (weights / total, (top + jnp.log(total))[..., 0])


def attend_forward(query, key, value, edge_mask, mid_mask, listed, blk, scale):
    heads_count, length, width = query.shape
    edge_scores = (
        jnp.einsum("hqd,hkd->hqk", edge_rows(query, blk), key, preferred_element_type=jnp.float32)
        * scale
    )
    edge_prob, edge_log = softmax_parts(edge_scores, edge_mask[None])
    edge_out = jnp.einsum(
        "hqk,hkd->hqd", edge_prob.astype(jnp.bfloat16), value, preferred_element_type=jnp.float32
    )
    near_key = near_blocks(key, listed, blk)
    near_value = near_blocks(value, listed, blk)
    mid_scores = (
        jnp.einsum(
            "hmqd,hmkd->hmqk", middle_rows(query, blk), near_key, preferred_element_type=jnp.float32
        )
        * scale
    )
    mid_prob, mid_log = softmax_parts(mid_scores, mid_mask)
    mid_out = jnp.einsum(
        "hmqk,hmkd->hmqd",
        mid_prob.astype(jnp.bfloat16),
        near_value,
        preferred_element_type=jnp.float32,
    )
    merged = jnp.concatenate(
        [
            edge_out[:, :blk],
            mid_out.reshape(heads_count, length - 2 * blk, width),
            edge_out[:, blk:],
        ],
        axis=1,
    )
    return (merged.astype(jnp.bfloat16), edge_log, mid_log)


def attend_backward(
    query, key, value, grad_out, edge_mask, mid_mask, edge_log, mid_log, listed, blk, scale
):
    heads_count, length, width = query.shape
    edge_query = edge_rows(query, blk)
    edge_grad = edge_rows(grad_out, blk)
    edge_scores = (
        jnp.einsum("hqd,hkd->hqk", edge_query, key, preferred_element_type=jnp.float32) * scale
    )
    edge_prob = jnp.exp(jnp.where(edge_mask[None], edge_scores, MASKED_SCORE) - edge_log[..., None])
    grad_value = jnp.einsum(
        "hqk,hqd->hkd",
        edge_prob.astype(jnp.bfloat16),
        edge_grad,
        preferred_element_type=jnp.float32,
    )
    edge_back = jnp.einsum("hqd,hkd->hqk", edge_grad, value, preferred_element_type=jnp.float32)
    edge_slope = (
        edge_prob * (edge_back - jnp.sum(edge_prob * edge_back, axis=-1, keepdims=True))
    ).astype(jnp.bfloat16)
    edge_grad_query = (
        jnp.einsum("hqk,hkd->hqd", edge_slope, key, preferred_element_type=jnp.float32) * scale
    )
    grad_key = (
        jnp.einsum("hqk,hqd->hkd", edge_slope, edge_query, preferred_element_type=jnp.float32)
        * scale
    )
    near_key = near_blocks(key, listed, blk)
    near_value = near_blocks(value, listed, blk)
    mid_query = middle_rows(query, blk)
    mid_grad = middle_rows(grad_out, blk)
    mid_scores = (
        jnp.einsum("hmqd,hmkd->hmqk", mid_query, near_key, preferred_element_type=jnp.float32)
        * scale
    )
    mid_prob = jnp.exp(jnp.where(mid_mask, mid_scores, MASKED_SCORE) - mid_log[..., None])
    near_grad_value = jnp.einsum(
        "hmqk,hmqd->hmkd",
        mid_prob.astype(jnp.bfloat16),
        mid_grad,
        preferred_element_type=jnp.float32,
    )
    mid_back = jnp.einsum(
        "hmqd,hmkd->hmqk", mid_grad, near_value, preferred_element_type=jnp.float32
    )
    mid_slope = (
        mid_prob * (mid_back - jnp.sum(mid_prob * mid_back, axis=-1, keepdims=True))
    ).astype(jnp.bfloat16)
    mid_grad_query = (
        jnp.einsum("hmqk,hmkd->hmqd", mid_slope, near_key, preferred_element_type=jnp.float32)
        * scale
    )
    near_grad_key = (
        jnp.einsum("hmqk,hmqd->hmkd", mid_slope, mid_query, preferred_element_type=jnp.float32)
        * scale
    )
    grad_key = grad_key + spread_blocks(near_grad_key, listed, blk, length)
    grad_value = grad_value + spread_blocks(near_grad_value, listed, blk, length)
    grad_query = jnp.concatenate(
        [
            edge_grad_query[:, :blk],
            mid_grad_query.reshape(heads_count, length - 2 * blk, width),
            edge_grad_query[:, blk:],
        ],
        axis=1,
    )
    return jnp.stack([grad_query, grad_key, grad_value]).astype(jnp.bfloat16)


def dot_rows(left, right):
    return jnp.dot(left, right, preferred_element_type=jnp.float32)


def dot_tokens(left, right):
    return lax.dot_general(
        left, right, (((0,), (0,)), ((), ())), preferred_element_type=jnp.float32
    )


def dot_back(left, right):
    return lax.dot_general(
        left, right, (((1,), (1,)), ((), ())), preferred_element_type=jnp.float32
    )


def forward_rows(act_low, weight):
    gathered = lax.all_gather(act_low, "row", axis=0, tiled=True)

    def term(start, count):
        return dot_rows(gathered, weight)

    return (
        gathered,
        lax.psum_scatter(
            term(jnp.int32(0), act_low.shape[0] * lax.axis_size("col")).astype(jnp.bfloat16),
            "col",
            scatter_dimension=0,
            tiled=True,
        ).astype(jnp.float32),
    )


def forward_cols(act_low, weight):
    gathered = lax.all_gather(act_low, "col", axis=0, tiled=True)

    def term(start, count):
        return dot_rows(gathered, weight)

    return (
        gathered,
        lax.psum_scatter(
            term(jnp.int32(0), act_low.shape[0] * lax.axis_size("row")).astype(jnp.bfloat16),
            "row",
            scatter_dimension=0,
            tiled=True,
        ).astype(jnp.float32),
    )


def backward_rows(grad_low, weight, gathered_in):
    grad_all = lax.all_gather(grad_low, "col", axis=0, tiled=True)
    weight_grad = dot_tokens(gathered_in, grad_all)
    bias_grad = jnp.sum(grad_all, axis=0, dtype=jnp.float32)

    def term(start, count):
        return dot_back(grad_all, weight)

    return (
        lax.psum_scatter(
            term(jnp.int32(0), grad_low.shape[0] * lax.axis_size("row")).astype(jnp.bfloat16),
            "row",
            scatter_dimension=0,
            tiled=True,
        ).astype(jnp.float32),
        weight_grad,
        bias_grad,
    )


def backward_cols(grad_low, weight, gathered_in):
    grad_all = lax.all_gather(grad_low, "row", axis=0, tiled=True)
    weight_grad = dot_tokens(gathered_in, grad_all)
    bias_grad = jnp.sum(grad_all, axis=0, dtype=jnp.float32)

    def term(start, count):
        return dot_back(grad_all, weight)

    return (
        lax.psum_scatter(
            term(jnp.int32(0), grad_low.shape[0] * lax.axis_size("col")).astype(jnp.bfloat16),
            "col",
            scatter_dimension=0,
            tiled=True,
        ).astype(jnp.float32),
        weight_grad,
        bias_grad,
    )


def norm_forward(value, gain, shift, width):
    sums = lax.psum((jnp.sum(value, axis=1), jnp.sum(value * value, axis=1)), "col")
    mean = sums[0][:, None] / width
    variance = sums[1][:, None] / width - mean * mean
    inverse = lax.rsqrt(variance + EPSILON)
    normed = (value - mean) * inverse
    return (normed * gain + shift, normed, inverse)


def norm_backward(grad_out, normed, inverse, gain, width):
    scaled = grad_out * gain
    sums = lax.psum((jnp.sum(scaled, axis=1), jnp.sum(scaled * normed, axis=1)), "col")
    grad_in = inverse * (scaled - sums[0][:, None] / width - normed * sums[1][:, None] / width)
    return (grad_in, jnp.sum(grad_out * normed, axis=0), jnp.sum(grad_out, axis=0))


def split_heads(project_low, seqs_count, length, heads_count, head_width):
    return project_low.reshape(seqs_count, length, 3, heads_count, head_width).transpose(
        0, 2, 3, 1, 4
    )


def layer_forward(hidden, params, listed, kept, segments, valid, width):
    (
        project_weight,
        project_bias,
        merge_weight,
        merge_bias,
        first_gain,
        first_shift,
        expand_weight,
        expand_bias,
        shrink_weight,
        shrink_bias,
        second_gain,
        second_shift,
    ) = params
    inner_width = project_weight.shape[2]
    gathered_in, project = forward_rows(
        hidden.astype(jnp.bfloat16), project_weight.reshape(project_weight.shape[0], -1)
    )
    full_bias = jnp.concatenate(
        [project_bias, jnp.zeros_like(project_bias), jnp.zeros_like(project_bias)]
    )
    project_low = (project + full_bias).astype(jnp.bfloat16)
    seqs_count, length = segments.shape
    heads_count = listed.shape[0]
    head_width = inner_width // heads_count
    parts = split_heads(project_low, seqs_count, length, heads_count, head_width)
    scale = head_width ** (-0.5)

    def per_sequence(inputs):
        part, segment, valid_one = inputs
        edge_mask, mid_mask = sequence_masks(segment, valid_one, listed, kept, BLK)
        return attend_forward(part[0], part[1], part[2], edge_mask, mid_mask, listed, BLK, scale)

    mixed, edge_log, mid_log = lax.map(per_sequence, (parts, segments, valid))
    mixed_low = mixed.transpose(0, 2, 1, 3).reshape(seqs_count * length, inner_width)
    gathered_mix, branch = forward_cols(mixed_low, merge_weight)
    first, first_hat, first_inverse = norm_forward(
        hidden + (branch + merge_bias), first_gain, first_shift, width
    )
    gathered_first, inner = forward_rows(first.astype(jnp.bfloat16), expand_weight)
    inner = inner + expand_bias
    active_low = jax.nn.gelu(inner, approximate=True).astype(jnp.bfloat16)
    gathered_active, second = forward_cols(active_low, shrink_weight)
    output, second_hat, second_inverse = norm_forward(
        first + (second + shrink_bias), second_gain, second_shift, width
    )
    saved = (
        gathered_in,
        project_low,
        edge_log,
        mid_log,
        gathered_mix,
        first_hat,
        first_inverse,
        gathered_first,
        inner,
        gathered_active,
        second_hat,
        second_inverse,
    )
    return (output, saved)


def layer_backward(grad_out, params, saved, listed, kept, segments, valid, width):
    (
        project_weight,
        project_bias,
        merge_weight,
        merge_bias,
        first_gain,
        first_shift,
        expand_weight,
        expand_bias,
        shrink_weight,
        shrink_bias,
        second_gain,
        second_shift,
    ) = params
    (
        gathered_in,
        project_low,
        edge_log,
        mid_log,
        gathered_mix,
        first_hat,
        first_inverse,
        gathered_first,
        inner,
        gathered_active,
        second_hat,
        second_inverse,
    ) = saved
    grad_second, second_gain_grad, second_shift_grad = norm_backward(
        grad_out, second_hat, second_inverse, second_gain, width
    )
    grad_active, shrink_grad, shrink_bias_grad = backward_cols(
        grad_second.astype(jnp.bfloat16), shrink_weight, gathered_active
    )
    gelu_value, gelu_pull = jax.vjp(partial(jax.nn.gelu, approximate=True), inner)
    grad_inner = gelu_pull(grad_active)[0].astype(jnp.bfloat16)
    grad_first_part, expand_grad, expand_bias_grad = backward_rows(
        grad_inner, expand_weight, gathered_first
    )
    grad_first, first_gain_grad, first_shift_grad = norm_backward(
        grad_second + grad_first_part, first_hat, first_inverse, first_gain, width
    )
    grad_mixed, merge_grad, merge_bias_grad = backward_cols(
        grad_first.astype(jnp.bfloat16), merge_weight, gathered_mix
    )
    seqs_count, length = segments.shape
    heads_count = listed.shape[0]
    inner_width = project_weight.shape[2]
    head_width = inner_width // heads_count
    scale = head_width ** (-0.5)
    parts = split_heads(project_low, seqs_count, length, heads_count, head_width)
    grad_heads = (
        grad_mixed.astype(jnp.bfloat16)
        .reshape(seqs_count, length, heads_count, head_width)
        .transpose(0, 2, 1, 3)
    )

    def per_sequence(inputs):
        part, grad_one, segment, valid_one, edge_one, mid_one = inputs
        edge_mask, mid_mask = sequence_masks(segment, valid_one, listed, kept, BLK)
        return attend_backward(
            part[0],
            part[1],
            part[2],
            grad_one,
            edge_mask,
            mid_mask,
            edge_one,
            mid_one,
            listed,
            BLK,
            scale,
        )

    grad_parts = lax.map(per_sequence, (parts, grad_heads, segments, valid, edge_log, mid_log))
    grad_project = grad_parts.transpose(0, 3, 1, 2, 4).reshape(seqs_count * length, 3 * inner_width)
    grad_in_part, project_grad, project_bias_grad = backward_rows(
        grad_project, project_weight.reshape(project_weight.shape[0], -1), gathered_in
    )
    project_grad = project_grad.reshape(project_weight.shape)
    project_bias_grad = project_bias_grad.reshape(3, inner_width)
    weight_grads = (
        project_grad[:, 0:2],
        project_grad[:, 2],
        project_bias_grad[0],
        merge_grad,
        merge_bias_grad,
        expand_grad,
        expand_bias_grad,
        shrink_grad,
        shrink_bias_grad,
    )
    gain_terms = (first_gain_grad, first_shift_grad, second_gain_grad, second_shift_grad)
    return (grad_first + grad_in_part, weight_grads, gain_terms)


def body(
    tokens_in,
    teacher,
    qkv_weight,
    query_bias,
    out_weight,
    out_bias,
    first_gain,
    first_shift,
    up_weight,
    up_bias,
    down_weight,
    down_bias,
    second_gain,
    second_shift,
    random_blocks,
    segment_ids,
    padding_mask,
):
    row_count = lax.axis_size("row")
    col_count = lax.axis_size("col")
    heads_local = random_blocks.shape[1] // row_count
    listed_all, kept_all = block_lists(random_blocks)
    listed_all = lax.dynamic_slice_in_dim(
        listed_all, lax.axis_index("row") * heads_local, heads_local, 1
    )
    kept_all = lax.dynamic_slice_in_dim(
        kept_all, lax.axis_index("row") * heads_local, heads_local, 1
    )
    seq_share = segment_ids.shape[0] // col_count
    attend_segments = lax.dynamic_slice_in_dim(
        segment_ids, lax.axis_index("col") * seq_share, seq_share, 0
    )
    attend_valid = lax.dynamic_slice_in_dim(
        padding_mask, lax.axis_index("col") * seq_share, seq_share, 0
    )
    row_share = padding_mask.shape[0] // row_count
    loss_valid = lax.dynamic_slice_in_dim(
        padding_mask, lax.axis_index("row") * row_share, row_share, 0
    ).reshape(-1)
    width = tokens_in.shape[1] * col_count
    layers_count = qkv_weight.shape[0]
    all_params = (
        qkv_weight,
        query_bias,
        out_weight,
        out_bias,
        first_gain,
        first_shift,
        up_weight,
        up_bias,
        down_weight,
        down_bias,
        second_gain,
        second_shift,
    )
    hidden = tokens_in.astype(jnp.float32)
    saved_all = []
    for layer in range(layers_count):
        params = tuple((item[layer] for item in all_params))
        hidden, saved = layer_forward(
            hidden, params, listed_all[layer], kept_all[layer], attend_segments, attend_valid, width
        )
        saved_all.append(saved)
    live = loss_valid.astype(jnp.float32)[:, None]
    error = hidden - teacher.astype(jnp.float32)
    partial_total = jnp.sum(live * error * error)
    partial_count = jnp.sum(live) / col_count
    total, count = lax.psum((partial_total, partial_count), ("dp", "row", "col"))
    loss = total / (width * count)
    tokens_all = hidden.shape[0] * row_count * lax.axis_size("dp")
    grad = live * error * (2.0 * tokens_all / count)
    weight_grads = [None] * layers_count
    gain_terms = [None] * layers_count
    for layer in reversed(range(layers_count)):
        params = tuple((item[layer] for item in all_params))
        grad, layer_weights, layer_gains = layer_backward(
            grad,
            params,
            saved_all[layer],
            listed_all[layer],
            kept_all[layer],
            attend_segments,
            attend_valid,
            width,
        )
        weight_grads[layer] = layer_weights
        gain_terms[layer] = layer_gains
    stacked = [jnp.stack([entry[member] for entry in weight_grads]) for member in range(9)]
    stacked = lax.psum(
        (
            stacked[0],
            stacked[1],
            stacked[2],
            stacked[3],
            stacked[4],
            stacked[5],
            stacked[6],
            stacked[7],
            stacked[8],
        ),
        "dp",
    )
    gains = [jnp.stack([entry[member] for entry in gain_terms]) for member in range(4)]
    gains = lax.psum((gains[0], gains[1], gains[2], gains[3]), ("dp", "row"))
    return (
        hidden,
        loss,
        grad,
        stacked[0],
        stacked[1],
        stacked[2],
        stacked[3],
        stacked[4],
        gains[0],
        gains[1],
        stacked[5],
        stacked[6],
        stacked[7],
        stacked[8],
        gains[2],
        gains[3],
    )


def solution(mesh):
    return jax.shard_map(
        body,
        mesh=mesh,
        in_specs=(
            P(("dp", "row"), "col"),
            P(("dp", "row"), "col"),
            P(None, "col", None, "row"),
            P(None, "row"),
            P(None, "row", "col"),
            P(None, "col"),
            P(None, "col"),
            P(None, "col"),
            P(None, "col", "row"),
            P(None, "row"),
            P(None, "row", "col"),
            P(None, "col"),
            P(None, "col"),
            P(None, "col"),
            P(),
            P("dp", None),
            P("dp", None),
        ),
        out_specs=(
            P(("dp", "row"), "col"),
            P(),
            P(("dp", "row"), "col"),
            P(None, "col", None, "row"),
            P(None, "col", "row"),
            P(None, "row"),
            P(None, "row", "col"),
            P(None, "col"),
            P(None, "col"),
            P(None, "col"),
            P(None, "col", "row"),
            P(None, "row"),
            P(None, "row", "col"),
            P(None, "col"),
            P(None, "col"),
            P(None, "col"),
        ),
        check_vma=False,
    )
```

profile of v0, /device:TPU:0, one launch (start us, length us, event | category | flops | bytes accessed | tf_op | source)
XLA Modules:
  0.0 3008.1 jit_solution(1807184456174210860)
XLA Ops:
  40.5 19.1 gather_fusion.6
  59.6 19.1 gather_fusion.4
  81.0 170.5 %gather_fusion.7 = s32[43008]{0:T(1024)S(1)} fusion(s32[1024]{0:T(1024)S(1)} %bitcast.341, s32[43008]{0:T(1024)S(1)} %broadcast_clamp_fusion.1), kind=kCustom, calls=%fused_computation.7 | custom fusion | bytes 516096 | tf_op jit(solution)/shard_map/while/body/eval_jaxpr/gather | solution.py:32
  251.5 170.5 %gather_fusion.5 = s32[43008]{0:T(1024)S(1)} fusion(s32[1024]{0:T(1024)S(1)} %bitcast.336, s32[43008]{0:T(1024)S(1)} %broadcast_clamp_fusion.1), kind=kCustom, calls=%fused_computation.5 | custom fusion | bytes 516096 | tf_op jit(solution)/shard_map/while/body/eval_jaxpr/gather | solution.py:31
  519.6 28.4 all-gather.19.cloned.1.call-done
  590.4 77.1 %reduce-scatter.21.cloned.1.call-done = bf16[1024,1536]{1,0:T(8,128)(2,1)} async-done(((bf16[2048,1536]{1,0:T(8,128)(2,1)}), bf16[1024,1536]{1,0:T(8,128)(2,1)}) %reduce-scatter.21.cloned.1.call-update) | async-done | bytes 3145744 | tf_op jit(solution)/shard_map/reduce_scatter | solution.py:222
  672.5 80.4 %all-gather.23.cloned.1.call-done = bf16[2048,1536]{1,0:T(8,128)(2,1)} async-done(((bf16[1024,1536]{1,0:T(8,128)(2,1)}), bf16[2048,1536]{1,0:T(8,128)(2,1)}) %all-gather.23.cloned.1.call-update) | async-done | bytes 6291472 | tf_op jit(solution)/shard_map/all_gather | solution.py:232
  797.6 170.5 %gather_fusion.9 = s32[43008]{0:T(1024)S(1)} fusion(s32[1024]{0:T(1024)S(1)} %bitcast.342, s32[43008]{0:T(1024)S(1)} %broadcast_clamp_fusion), kind=kCustom, calls=%fused_computation.9 | custom fusion | bytes 516096 | tf_op jit(solution)/shard_map/while/body/eval_jaxpr/gather | solution.py:32
  968.2 170.5 %gather_fusion.8 = s32[43008]{0:T(1024)S(1)} fusion(s32[1024]{0:T(1024)S(1)} %bitcast.337, s32[43008]{0:T(1024)S(1)} %broadcast_clamp_fusion), kind=kCustom, calls=%fused_computation.8 | custom fusion | bytes 516096 | tf_op jit(solution)/shard_map/while/body/eval_jaxpr/gather | solution.py:31
  1230.0 28.4 all-gather.27.cloned.1.call-done
  1298.6 78.3 %reduce-scatter.29.cloned.1.call-done = bf16[1024,1536]{1,0:T(8,128)(2,1)} async-done(((bf16[2048,1536]{1,0:T(8,128)(2,1)}), bf16[1024,1536]{1,0:T(8,128)(2,1)}) %reduce-scatter.29.cloned.1.call-update) | async-done | bytes 3145744 | tf_op jit(solution)/shard_map/reduce_scatter | solution.py:222
  1382.4 80.0 %all-gather.31.cloned.1.call-done = bf16[2048,1536]{1,0:T(8,128)(2,1)} async-done(((bf16[1024,1536]{1,0:T(8,128)(2,1)}), bf16[2048,1536]{1,0:T(8,128)(2,1)}) %all-gather.31.cloned.1.call-update) | async-done | bytes 6291472 | tf_op jit(solution)/shard_map/all_gather | solution.py:232
  1489.5 40.8 %all-reduce.2 = (f32[]{:T(128)}, f32[]{:T(128)}) all-reduce(f32[]{:T(128)} %get-tuple-element.244, f32[]{:T(128)S(6)} %div.121), channel_id=1, replica_groups=mesh['dp'=8,'row'=2,'col'=2] {'dp','row','col'}, use_global_device_ids=true, to_apply=%region_34.35 | all-reduce | flops 2 | bytes 16 | tf_op jit(solution)/shard_map/psum | solution.py:539
  1560.7 78.3 %reduce-scatter.33.cloned.1.call-done = bf16[1024,1536]{1,0:T(8,128)(2,1)} async-done(((bf16[2048,1536]{1,0:T(8,128)(2,1)}), bf16[1024,1536]{1,0:T(8,128)(2,1)}) %reduce-scatter.33.cloned.1.call-update) | async-done | bytes 3145744 | tf_op jit(solution)/shard_map/reduce_scatter | solution.py:277
  1647.2 80.3 %all-gather.35.cloned.1.call-done = bf16[2048,1536]{1,0:T(8,128)(2,1)} async-done(((bf16[1024,1536]{1,0:T(8,128)(2,1)}), bf16[2048,1536]{1,0:T(8,128)(2,1)}) %all-gather.35.cloned.1.call-update) | async-done | bytes 6291472 | tf_op jit(solution)/shard_map/all_gather | solution.py:249
  1770.5 26.7 reduce-scatter.37.cloned.1.call-done
  1840.6 16.6 reshape.827
  1857.2 30.8 %fusion.48 = f32[6,16,64,64]{2,1,3,0:T(8,128)} fusion(f32[6,14,8,64,64]{3,2,4,1,0:T(8,128)} %reshape.827, s32[6,14,8]{1,2,0:T(8,128)S(1)} %copy-done.68), kind=kOutput, calls=%fused_computation.133 | convolution fusion | flops 528493056 | bytes 12585600 | tf_op jit(solution)/shard_map/while/body/eval_jaxpr/hmjb,hmjtw->hbtw/dot_general | solution.py:72
  1895.0 16.6 reshape.829
  1911.6 30.5 %fusion.51 = f32[6,16,64,64]{2,1,3,0:T(8,128)} fusion(f32[6,14,8,64,64]{3,2,4,1,0:T(8,128)} %reshape.829, s32[6,14,8]{1,2,0:T(8,128)S(1)} %copy-done.68), kind=kOutput, calls=%fused_computation.134 | convolution fusion | flops 528493056 | bytes 12585600 | tf_op jit(solution)/shard_map/while/body/eval_jaxpr/hmjb,hmjtw->hbtw/dot_general | solution.py:72
  1950.8 62.3 %all-gather.39.cloned.1.call-done = bf16[2048,1152]{0,1:T(8,128)(2,1)} async-done(((bf16[1024,1152]{0,1:T(8,128)(2,1)}), bf16[2048,1152]{0,1:T(8,128)(2,1)}) %all-gather.39.cloned.1.call-update) | async-done | bytes 4718608 | tf_op jit(solution)/shard_map/all_gather | solution.py:249
  2058.4 78.3 %reduce-scatter.41.cloned.1.call-done = bf16[1024,1536]{1,0:T(8,128)(2,1)} async-done(((bf16[2048,1536]{1,0:T(8,128)(2,1)}), bf16[1024,1536]{1,0:T(8,128)(2,1)}) %reduce-scatter.41.cloned.1.call-update) | async-done | bytes 3145744 | tf_op jit(solution)/shard_map/reduce_scatter | solution.py:277
  2144.3 80.4 %all-gather.43.cloned.1.call-done = bf16[2048,1536]{1,0:T(8,128)(2,1)} async-done(((bf16[1024,1536]{1,0:T(8,128)(2,1)}), bf16[2048,1536]{1,0:T(8,128)(2,1)}) %all-gather.43.cloned.1.call-update) | async-done | bytes 6291472 | tf_op jit(solution)/shard_map/all_gather | solution.py:249
  2268.1 26.7 reduce-scatter.45.cloned.1.call-done
  2341.1 16.6 reshape.835
  2357.7 30.6 %fusion.54 = f32[6,16,64,64]{2,1,3,0:T(8,128)} fusion(f32[6,14,8,64,64]{3,2,4,1,0:T(8,128)} %reshape.835, s32[6,14,8]{1,2,0:T(8,128)S(1)} %copy-done.66), kind=kOutput, calls=%fused_computation.135 | convolution fusion | flops 528493056 | bytes 12585600 | tf_op jit(solution)/shard_map/while/body/eval_jaxpr/hmjb,hmjtw->hbtw/dot_general | solution.py:72
  2395.3 16.6 reshape.837
  2411.9 30.8 %fusion.57 = f32[6,16,64,64]{2,1,3,0:T(8,128)} fusion(f32[6,14,8,64,64]{3,2,4,1,0:T(8,128)} %reshape.837, s32[6,14,8]{1,2,0:T(8,128)S(1)} %copy-done.66), kind=kOutput, calls=%fused_computation.136 | convolution fusion | flops 528493056 | bytes 12585600 | tf_op jit(solution)/shard_map/while/body/eval_jaxpr/hmjb,hmjtw->hbtw/dot_general | solution.py:72
  2476.2 37.4 %all-gather.47.cloned.1.call-done = bf16[2048,1152]{0,1:T(8,128)(2,1)} async-done(((bf16[1024,1152]{0,1:T(8,128)(2,1)}), bf16[2048,1152]{0,1:T(8,128)(2,1)}) %all-gather.47.cloned.1.call-update) | async-done | bytes 4718608 | tf_op jit(solution)/shard_map/all_gather | solution.py:249
  2553.4 65.5 %all-reduce.3 = (f32[2,384]{1,0:T(2,128)}, f32[2,384]{1,0:T(2,128)}, f32[2,384]{1,0:T(2,128)}, f32[2,384]{1,0:T(2,128)}) all-reduce(f32[2,384]{1,0:T(2,128)S(1)} %pad_maximum_fusion.24, f32[2,384]{1,0:T(2,128)S(1)} %pad_maximum_fusion.25, f32[2,384]{1,0:T(2,128)S(1)} %pad_maximum_fusion.27, ...), channel_id=1, replica_groups=mesh['dp'=8,'row'=2,'col'=2] {'dp','row'}, use_global_device_ids=true, to_apply=%region_76.77 | all-reduce | flops 3072 | bytes 24576 | tf_op jit(solution)/shard_map/psum | solution.py:575
  2622.3 36.0 %all-reduce.4 = (f32[2,384]{1,0:T(2,128)}, f32[2,384]{1,0:T(2,128)}, f32[2,1536]{1,0:T(2,128)}, f32[2,384]{1,0:T(2,128)}) all-reduce(f32[2,384]{1,0:T(2,128)S(1)} %pad_maximum_fusion.22, f32[2,384]{1,0:T(2,128)S(1)} %pad_maximum_fusion.23, f32[2,1536]{1,0:T(2,128)S(1)} %pad_maximum_fusion.21, ...), channel_id=1, replica_groups=mesh['dp'=8,'row'=2,'col'=2] {'dp'}, use_global_device_ids=true, to_apply=%region_69.70 | all-reduce | flops 5376 | bytes 43008 | tf_op jit(solution)/shard_map/psum | solution.py:560
  2660.8 323.6 %all-reduce.16.cloned.1.call-done = (f32[2,384,2,384]{1,3,2,0:T(8,128)}, f32[2,384,384]{1,2,0:T(8,128)}, f32[2,384,384]{2,1,0:T(8,128)}, f32[2,384,1536]{2,1,0:T(8,128)}, f32[2,1536,384]{2,1,0:T(8,128)}) async-done(((f32[2,384,2,384]{1,3,2,0:T(8,128)}, f32[2,384,384]{1,2,0:T(8,128)}, f32[2,384,384]{2,1,0:T(8,128)}, f32[2,384,1536]{2,1,0:T(8,128)}, f32[2,1536,384]{2,1,0:T(8,128)}), ...) | async-done | bytes 14155792 | tf_op jit(solution)/shard_map/psum | solution.py:560
  (727 shorter events, 768.5 us)
Async XLA Ops:
  7.9 421.2 %reduce-scatter.17.cloned.1.call-start = ((), (), s32[]{:S(2)}) async-start(), calls=%async_computation.17 | async-start | bytes 7077888 | tf_op jit(solution)/shard_map/reduce_scatter | solution.py:222
  28.5 519.5 %all-gather.19.cloned.1.call-start = ((), (), s32[]{:S(2)}) async-start(), calls=%async_computation.18 | async-start | bytes 2359296 | tf_op jit(solution)/shard_map/all_gather | solution.py:232
  519.5 41.5 %reduce-scatter.19.cloned.1.call-start = ((), (), s32[]{:S(2)}) async-start(), calls=%async_computation.19 | async-start | bytes 2359296 | tf_op jit(solution)/shard_map/reduce_scatter | solution.py:239
  551.7 29.5 all-gather.21.cloned.1.call-start
  570.1 97.4 %reduce-scatter.21.cloned.1.call-start = ((), (), s32[]{:S(2)}) async-start(), calls=%async_computation.21 | async-start | bytes 9437184 | tf_op jit(solution)/shard_map/reduce_scatter | solution.py:222
  589.1 163.9 %all-gather.23.cloned.1.call-start = ((), (), s32[]{:S(2)}) async-start(), calls=%async_computation.22 | async-start | bytes 9437184 | tf_op jit(solution)/shard_map/all_gather | solution.py:232
  672.5 97.4 %reduce-scatter.23.cloned.1.call-start = ((), (), s32[]{:S(2)}) async-start(), calls=%async_computation.23 | async-start | bytes 2359296 | tf_op jit(solution)/shard_map/reduce_scatter | solution.py:239
  760.6 29.6 all-gather.25.cloned.1.call-start
  779.1 361.7 %reduce-scatter.25.cloned.1.call-start = ((), (), s32[]{:S(2)}) async-start(), calls=%async_computation.25 | async-start | bytes 7077888 | tf_op jit(solution)/shard_map/reduce_scatter | solution.py:222
  796.7 461.8 %all-gather.27.cloned.1.call-start = ((), (), s32[]{:S(2)}) async-start(), calls=%async_computation.26 | async-start | bytes 2359296 | tf_op jit(solution)/shard_map/all_gather | solution.py:232
  1229.9 41.4 %reduce-scatter.27.cloned.1.call-start = ((), (), s32[]{:S(2)}) async-start(), calls=%async_computation.27 | async-start | bytes 2359296 | tf_op jit(solution)/shard_map/reduce_scatter | solution.py:239
  1262.2 28.5 all-gather.29.cloned.1.call-start
  1279.5 97.4 %reduce-scatter.29.cloned.1.call-start = ((), (), s32[]{:S(2)}) async-start(), calls=%async_computation.29 | async-start | bytes 9437184 | tf_op jit(solution)/shard_map/reduce_scatter | solution.py:222
  1298.5 163.9 %all-gather.31.cloned.1.call-start = ((), (), s32[]{:S(2)}) async-start(), calls=%async_computation.30 | async-start | bytes 9437184 | tf_op jit(solution)/shard_map/all_gather | solution.py:232
  1381.9 97.4 %reduce-scatter.31.cloned.1.call-start = ((), (), s32[]{:S(2)}) async-start(), calls=%async_computation.31 | async-start | bytes 2359296 | tf_op jit(solution)/shard_map/reduce_scatter | solution.py:239
  1470.1 82.7 %all-gather.33.cloned.1.call-start = ((), (), s32[]{:S(2)}) async-start(), calls=%async_computation.32 | async-start | bytes 2359296 | tf_op jit(solution)/shard_map/all_gather | solution.py:269
  1543.3 95.8 %reduce-scatter.33.cloned.1.call-start = ((), (), s32[]{:S(2)}) async-start(), calls=%async_computation.33 | async-start | bytes 9437184 | tf_op jit(solution)/shard_map/reduce_scatter | solution.py:277
  1560.7 166.9 %all-gather.35.cloned.1.call-start = ((), (), s32[]{:S(2)}) async-start(), calls=%async_computation.34 | async-start | bytes 9437184 | tf_op jit(solution)/shard_map/all_gather | solution.py:249
  1647.0 97.5 %reduce-scatter.35.cloned.1.call-start = ((), (), s32[]{:S(2)}) async-start(), calls=%async_computation.35 | async-start | bytes 2359296 | tf_op jit(solution)/shard_map/reduce_scatter | solution.py:257
  1735.3 30.9 %all-gather.37.cloned.1.call-start = ((), (), s32[]{:S(2)}) async-start(), calls=%async_computation.36 | async-start | bytes 2359296 | tf_op jit(solution)/shard_map/all_gather | solution.py:269
  1755.0 42.3 %reduce-scatter.37.cloned.1.call-start = ((), (), s32[]{:S(2)}) async-start(), calls=%async_computation.37 | async-start | bytes 2359296 | tf_op jit(solution)/shard_map/reduce_scatter | solution.py:277
  1769.9 243.2 %all-gather.39.cloned.1.call-start = ((), (), s32[]{:S(2)}) async-start(), calls=%async_computation.38 | async-start | bytes 7077888 | tf_op jit(solution)/shard_map/all_gather | solution.py:249
  1950.3 78.5 %reduce-scatter.39.cloned.1.call-start = ((), (), s32[]{:S(2)}) async-start(), calls=%async_computation.39 | async-start | bytes 2359296 | tf_op jit(solution)/shard_map/reduce_scatter | solution.py:257
  2019.6 30.9 %all-gather.41.cloned.1.call-start = ((), (), s32[]{:S(2)}) async-start(), calls=%async_computation.40 | async-start | bytes 2359296 | tf_op jit(solution)/shard_map/all_gather | solution.py:269
  2039.3 97.4 %reduce-scatter.41.cloned.1.call-start = ((), (), s32[]{:S(2)}) async-start(), calls=%async_computation.41 | async-start | bytes 9437184 | tf_op jit(solution)/shard_map/reduce_scatter | solution.py:277
  2058.4 166.4 %all-gather.43.cloned.1.call-start = ((), (), s32[]{:S(2)}) async-start(), calls=%async_computation.42 | async-start | bytes 9437184 | tf_op jit(solution)/shard_map/all_gather | solution.py:249
  2144.3 97.4 %reduce-scatter.43.cloned.1.call-start = ((), (), s32[]{:S(2)}) async-start(), calls=%async_computation.43 | async-start | bytes 2359296 | tf_op jit(solution)/shard_map/reduce_scatter | solution.py:257
  2232.5 31.2 %all-gather.45.cloned.1.call-start = ((), (), s32[]{:S(2)}) async-start(), calls=%async_computation.44 | async-start | bytes 2359296 | tf_op jit(solution)/shard_map/all_gather | solution.py:269
  2252.5 42.2 %reduce-scatter.45.cloned.1.call-start = ((), (), s32[]{:S(2)}) async-start(), calls=%async_computation.45 | async-start | bytes 2359296 | tf_op jit(solution)/shard_map/reduce_scatter | solution.py:277
  2267.4 246.3 %all-gather.47.cloned.1.call-start = ((), (), s32[]{:S(2)}) async-start(), calls=%async_computation.46 | async-start | bytes 7077888 | tf_op jit(solution)/shard_map/all_gather | solution.py:249
  2450.8 207.6 %reduce-scatter.47.cloned.1.call-start = ((), (), s32[]{:S(2)}) async-start(), calls=%async_computation.47 | async-start | bytes 2359296 | tf_op jit(solution)/shard_map/reduce_scatter | solution.py:257
  2520.2 464.1 %all-reduce.16.cloned.1.call-start = ((), (), s32[]{:S(2)}) async-start(), calls=%async_computation.48 | async-start | bytes 28311552 | tf_op jit(solution)/shard_map/psum | solution.py:560
  (177 other events, 4963.4 us)
Sparse Core Ops, SparseCore 0:
  9.6 12.4 all-gather.16
  28.6 61.1 reduce-scatter.16
  519.6 28.3 all-gather.18
  551.9 9.0 reduce-scatter.18
  570.2 11.0 all-gather.20
  589.2 78.2 reduce-scatter.20
  672.6 80.3 all-gather.22
  760.8 9.0 reduce-scatter.22
  779.2 11.0 all-gather.24
  796.8 61.1 reduce-scatter.24
  1230.0 28.3 all-gather.26
  1262.3 9.0 reduce-scatter.26
  1279.6 11.0 all-gather.28
  1298.6 78.2 reduce-scatter.28
  1382.0 80.3 all-gather.30
  1470.2 9.0 reduce-scatter.30
  1543.4 9.3 all-gather.32
  1560.8 78.2 reduce-scatter.32
  1647.1 80.3 all-gather.34
  1735.4 9.0 reduce-scatter.34
  1755.1 10.9 all-gather.36
  1770.0 27.2 reduce-scatter.36
  1950.4 62.6 all-gather.38
  2019.7 9.0 reduce-scatter.38
  2039.4 11.0 all-gather.40
  2058.5 78.2 reduce-scatter.40
  2144.3 80.3 all-gather.42
  2252.6 10.9 all-gather.44
  2267.5 27.2 reduce-scatter.44
  2451.0 62.6 all-gather.46
  2520.4 9.0 reduce-scatter.46
  2542.0 442.3 all-reduce.15
  (1 shorter events, 9.0 us)
where the time goes:
time: 3020 us; the launch traced here: 3010 us
  waiting for transfers between devices  1310 us (43%)
  local copies, waits for them, and re-layouts  978 us (32%)
  matrix products  382 us (13%)
  blocking collectives  183 us (6%)
  other arithmetic  130 us (4%)
    gather x8, local copies, waits for them, and re-layouts, allowed_pairs(): same = segment[query_pos][..., :, None] == segment[key_pos][..., None, :]  367 us
    gather x3, local copies, waits for them, and re-layouts, allowed_pairs(): valid[key_pos] > 0  346 us
    psum x1, waiting for transfers between devices, body(): lax.psum((stacked[0], stacked[1], stacked[2], stacked[3], stacked[4], sta...  324 us
    all_gather x4, waiting for transfers between devices, backward_rows(): grad_all = lax.all_gather(grad_low, 'col', axis=0, tiled=True)  261 us
    all_gather x4, waiting for transfers between devices, forward_cols(): gathered = lax.all_gather(act_low, 'col', axis=0, tiled=True)  217 us
    reduce_scatter x4, waiting for transfers between devices, backward_cols(): lax.psum_scatter(term(jnp.int32(0), grad_low.shape[0] * lax.axis_size('co...  210 us
    reduce_scatter x4, waiting for transfers between devices, forward_rows(): lax.psum_scatter(term(jnp.int32(0), act_low.shape[0] * lax.axis_size('col...  155 us
    dot_general x4, matrix products, spread_blocks(): jnp.einsum('hmjb,hmjtw->hbtw', chooser, pieces, precision=lax.Precision.H...  123 us
  transfers between devices with their start and end apart: 33, of which 30 were waited for; matrix products, arithmetic and copies ran while one was open for 27% of the time, Pallas kernels for 0%

commit v1 on v0

v1 whole, which is shorter than its diff:
```python
from functools import partial
from types import SimpleNamespace

import jax
import jax.numpy as jnp
from jax import lax
from jax.experimental import pallas as pl
from jax.experimental.pallas import tpu as pltpu
from jax.sharding import PartitionSpec as P

BLK = 64
EPSILON = 1e-06
MASKED_SCORE = -1e30
LANES = 128
SMALL_SLOTS = 8
TOKEN_BLOCK = 256
QKV, OUT, UP, DOWN, OUT_QKV, QKV_REST = range(6)
WHOLE, ROWS, SUM = -1, -2, -3
SCATTER, ADD, GATHER = range(3)
DP, ROW, COL = "dp", "row", "col"
VMEM_LIMIT = 48 * 1024 * 1024
GELU_SCALE = (2.0 / 3.141592653589793) ** 0.5
GELU_CUBE = 0.044715
BF16 = jnp.bfloat16
F32 = jnp.float32


def after(value, *before):
    return lax.optimization_barrier((value,) + before)[0]


def swap(value, axis):
    return lax.ppermute(value, axis, [(0, 1), (1, 0)])


def swap_bit(value, bit):
    count = lax.axis_size(DP)
    return lax.ppermute(value, DP, [(i, i ^ (1 << bit)) for i in range(count)])


def dp_bits():
    return (lax.axis_size(DP) - 1).bit_length()


def own_half(value, bit):
    halves = value.reshape(2, value.shape[0] // 2, value.shape[1])
    place = (lax.axis_index(DP) >> bit) & 1
    mine = lax.dynamic_index_in_dim(halves, place, 0, keepdims=False)
    other = lax.dynamic_index_in_dim(halves, 1 - place, 0, keepdims=False)
    return mine, other


def join_halves(mine, other, bit):
    place = (lax.axis_index(DP) >> bit) & 1
    return jnp.where(
        place == 0,
        jnp.concatenate([mine, other], axis=0),
        jnp.concatenate([other, mine], axis=0),
    )


class Line:
    def __init__(self):
        self.last = ()

    def next(self, value):
        return after(value, *self.last) if self.last else value

    def mark(self, *values):
        self.last = values
        return values[0]


class Fetch:
    def __init__(self, line, stack, layer, bit):
        self.bit = min(bit, dp_bits() - 1)
        half = stack.shape[1] // 2
        place = (lax.axis_index(DP) >> self.bit) & 1
        halves = line.next(stack).reshape((-1, half) + stack.shape[2:])
        piece = lax.dynamic_index_in_dim(halves, 2 * layer + place, 0, keepdims=False).reshape(half, -1)
        self.pieces = [swap(line.mark(piece), COL)]

    def pass_on(self, line):
        self.pieces[0] = line.mark(line.next(self.pieces[0]))
        self.pieces.append(swap_bit(self.pieces[0], self.bit))


class Reduce:
    def __init__(self, other, wide):
        self.got, self.joins, self.parts = swap(other, COL), None, None
        bits = dp_bits()
        if wide and bits > 2:
            middle = [(SCATTER, 1)] + [(ADD, bit) for bit in range(2, bits)] + [(GATHER, 1)]
        else:
            middle = [(ADD, bit) for bit in range(1, bits)]
        self.plan = [(SCATTER, 0)] + middle + [(GATHER, 0)]

    def done(self):
        return not self.plan

    def step(self, line):
        if self.done():
            return
        got = line.next(self.got)
        if self.joins is not None:
            parts = [join_halves(self.sent, got, self.joins)]
        else:
            parts = (self.parts or [self.own]) + [got]
        (kind, bit), self.plan = self.plan[0], self.plan[1:]
        self.joins = None
        if kind == SCATTER:
            halves = [own_half(part, bit) for part in parts]
            self.parts = [mine for mine, _ in halves]
            parts = [other for _, other in halves]
        self.sent = sum(part.astype(F32) for part in parts).astype(BF16)
        if kind == ADD:
            self.parts = [self.sent]
        elif kind == GATHER:
            self.joins = bit
        self.got = swap_bit(line.mark(self.sent), bit)

    def halves(self):
        return self.sent, self.got

    def collect(self, line):
        self.got = line.mark(line.next(self.got))


def attention_tables(segment, valid, random_blocks, pair_heads):
    layers, heads, middle, extra = random_blocks.shape
    length = segment.shape[0]
    blocks = length // BLK
    position = jnp.arange(length, dtype=jnp.int32)
    codes = jnp.where(valid > 0, segment, length + position)
    index = jnp.arange(1, blocks - 1, dtype=jnp.int32)
    window = jnp.stack(
        [jnp.zeros_like(index), jnp.full_like(index, blocks - 1), index - 1, index, index + 1],
        axis=1,
    )
    window = jnp.broadcast_to(window, random_blocks.shape[:-1] + (5,))
    listed = jnp.concatenate([window, random_blocks], axis=-1)
    total = listed.shape[-1]
    earlier = jnp.arange(total)[:, None] > jnp.arange(total)[None, :]
    kept = ~jnp.any((listed[..., :, None] == listed[..., None, :]) & earlier, axis=-1)
    real = (valid > 0).reshape(blocks, BLK)
    ids = segment.reshape(blocks, BLK)
    big = jnp.int32(1 << 20)
    low = jnp.min(jnp.where(real, ids, big), axis=1)
    high = jnp.max(jnp.where(real, ids, -big), axis=1)
    live = (low[:, None] <= high[None, :]) & (low[None, :] <= high[:, None])
    live = live | (jnp.arange(blocks)[:, None] == jnp.arange(blocks)[None, :])
    chosen = listed[..., None] == jnp.arange(blocks, dtype=jnp.int32)
    kept = kept & jnp.any(chosen & live[1 : blocks - 1][:, None, :], axis=-1)
    pairs = heads // pair_heads
    listed = listed.reshape(layers, pairs, pair_heads, middle, total)
    kept = kept.reshape(layers, pairs, pair_heads, middle, total)
    shared = [listed[:, :, 0, :, :5]] + [listed[:, :, h, :, 5:] for h in range(pair_heads)]
    used = [kept[:, :, 0, :, :5]] + [kept[:, :, h, :, 5:] for h in range(pair_heads)]
    shared, used = jnp.concatenate(shared, axis=-1), jnp.concatenate(used, axis=-1)
    slots = 5 + extra * pair_heads
    which = [0] * 5
    for h in range(pair_heads):
        which += [h + 1] * extra
    which = jnp.broadcast_to(jnp.array(which, jnp.int32), shared.shape)
    entry = shared | (jnp.where(used, shared, blocks) << 8) | (which << 16)
    sums = jnp.cumsum(used.astype(jnp.int32), axis=-1)
    count = sums[..., -1]
    spare = jnp.cumsum((~used).astype(jnp.int32), axis=-1)
    rank = jnp.where(used, sums - 1, count[..., None] + spare - 1)
    hot = rank[..., None, :] == jnp.arange(slots, dtype=jnp.int32)[:, None]
    entry = jnp.sum(jnp.where(hot, entry[..., None, :], 0), axis=-1, dtype=jnp.int32)
    most = jnp.max(count, axis=-1).astype(jnp.int32)
    code_blk = jnp.concatenate([codes.reshape(blocks, BLK)] * (LANES // BLK), axis=1)
    code_key = jnp.concatenate([codes, jnp.full((BLK,), -1, jnp.int32)])
    code_key = jnp.broadcast_to(code_key[:, None], (length + BLK, LANES))
    return [(entry[i], most[i], code_key, code_blk) for i in range(layers)]


def dot_nt(left, right):
    return lax.dot_general(left, right, (((1,), (1,)), ((), ())), preferred_element_type=F32)


def dot_nn(left, right):
    return lax.dot_general(left, right, (((1,), (0,)), ((), ())), preferred_element_type=F32)


def dot_tn(left, right):
    return lax.dot_general(left, right, (((0,), (0,)), ((), ())), preferred_element_type=F32)


def first_head(rows):
    return lax.broadcasted_iota(jnp.int32, (rows, LANES), 1) < BLK


def stacked(value, first):
    zero = jnp.zeros_like(value)
    return jnp.concatenate([jnp.where(first, value, zero), jnp.where(first, zero, value)], axis=0)


def block_rows(block):
    return pl.ds(pl.multiple_of(block * BLK, BLK), BLK)


def slot_entries(slot_ref, pair, block, count):
    words = [slot_ref[pair, block - 1, s] for s in range(count)]
    return [(word & 255, (word >> 8) & 255, word >> 16) for word in words]


def picked(ref, entries):
    return jnp.concatenate([ref[block_rows(entry[0]), :] for entry in entries], axis=0)


def visible(code_key_ref, code_row, entries):
    first = first_head(1)
    pieces = []
    for _, place, which in entries:
        row = jnp.where((which == 1) & ~first | (which == 2) & first, -2, code_row)
        pieces.append(code_key_ref[block_rows(place), :] == row)
    return jnp.concatenate(pieces, axis=0)


def middle_blocks(blocks, slots, most, work):
    small = min(SMALL_SLOTS, slots)

    @pl.when(most <= small)
    def _():
        for block in range(1, blocks - 1):
            work(block, small)

    @pl.when(most > small)
    def _():
        def body(block, carry):
            work(block, slots)
            return carry

        lax.fori_loop(1, blocks - 1, body, 0, unroll=2)


def forward_kernel(slot_ref, most_ref, q_ref, k_ref, v_ref, code_key_ref, code_blk_ref, out_ref, lse_ref, *, scale):
    pair = pl.program_id(0)
    blocks = q_ref.shape[0] // BLK
    first = first_head(BLK)

    def rows(block, keys, values, mask):
        at = block_rows(block)
        query = stacked(q_ref[at, :] * jnp.asarray(scale, BF16), first)
        scores = jnp.where(mask, dot_nt(keys, query), MASKED_SCORE)
        top = jnp.max(scores, axis=0, keepdims=True)
        weights = jnp.exp(scores - top)
        total = jnp.sum(weights, axis=0, keepdims=True)
        mixed = dot_tn((weights * (1.0 / total)).astype(BF16), values)
        out_ref[at, :] = jnp.where(first, mixed[:BLK], mixed[BLK:]).astype(BF16)
        lse_ref[0, pl.ds(block, 1), :] = top + jnp.log(total)

    for block in (0, blocks - 1):
        mask = code_key_ref[0 : blocks * BLK, :] == code_blk_ref[pl.ds(block, 1), :]
        rows(block, k_ref[...], v_ref[...], mask)

    def work(block, count):
        entries = slot_entries(slot_ref, pair, block, count)
        mask = visible(code_key_ref, code_blk_ref[pl.ds(block, 1), :], entries)
        rows(block, picked(k_ref, entries), picked(v_ref, entries), mask)

    middle_blocks(blocks, slot_ref.shape[2], most_ref[pair], work)


def backward_kernel(
    slot_ref,
    most_ref,
    q_ref,
    k_ref,
    v_ref,
    mixed_ref,
    grad_ref,
    lse_ref,
    code_key_ref,
    code_blk_ref,
    out_ref,
    dk_ref,
    dv_ref,
    *,
    scale,
    start,
):
    step = pl.program_id(0)
    pair = step + start
    blocks = q_ref.shape[0] // BLK
    width = out_ref.shape[1] // 3
    first = first_head(BLK)
    ones = jnp.ones((8, LANES), F32)

    def column(kind):
        return pl.ds(pl.multiple_of(kind * width + step * LANES, LANES), LANES)

    def rows(block, keys, values, mask):
        at = block_rows(block)
        query = stacked(q_ref[at, :] * jnp.asarray(scale, BF16), first)
        grad = grad_ref[at, :]
        along = stacked(grad.astype(F32) * mixed_ref[at, :].astype(F32), first)
        along = lax.dot_general(
            ones, along, (((1,), (1,)), ((), ())), precision=lax.Precision.HIGHEST, preferred_element_type=F32
        )[0:1]
        grad = stacked(grad, first)
        prob = jnp.where(mask, jnp.exp(dot_nt(keys, query) - lse_ref[0, pl.ds(block, 1), :]), 0.0)
        slope = (prob * (dot_nt(values, grad) - along)).astype(BF16)
        back = dot_tn(keys, slope).T
        out_ref[at, column(0)] = (jnp.where(first, back[:BLK], back[BLK:]) * scale).astype(BF16)
        return dot_nn(slope, query), dot_nn(prob.astype(BF16), grad)

    def edge(block):
        mask = code_key_ref[0 : blocks * BLK, :] == code_blk_ref[pl.ds(block, 1), :]
        return rows(block, k_ref[...], v_ref[...], mask)

    dk, dv = edge(0)
    dk_ref[...] = dk
    dv_ref[...] = dv
    dk, dv = edge(blocks - 1)
    dk_ref[...] += dk
    dv_ref[...] += dv

    def work(block, count):
        entries = slot_entries(slot_ref, pair, block, count)
        mask = visible(code_key_ref, code_blk_ref[pl.ds(block, 1), :], entries)
        dk, dv = rows(block, picked(k_ref, entries), picked(v_ref, entries), mask)
        for s, entry in enumerate(entries):
            at = block_rows(entry[0])
            dk_ref[at, :] += dk[s * BLK : (s + 1) * BLK]
            dv_ref[at, :] += dv[s * BLK : (s + 1) * BLK]

    middle_blocks(blocks, slot_ref.shape[2], most_ref[pair], work)
    out_ref[:, column(1)] = dk_ref[...].astype(BF16)
    out_ref[:, column(2)] = dv_ref[...].astype(BF16)


def whole_block(shape):
    return pl.BlockSpec(shape, lambda p, *_: (0,) * len(shape))


def attend_forward(project_low, tables, scale):
    entry, most, code_key, code_blk = tables
    length = project_low.shape[0]
    pairs = project_low.shape[1] // (3 * LANES)
    blocks = length // BLK

    def column(kind):
        return pl.BlockSpec((length, LANES), lambda p, *_: (0, kind * pairs + p))

    return pl.pallas_call(
        partial(forward_kernel, scale=scale),
        grid_spec=pltpu.PrefetchScalarGridSpec(
            num_scalar_prefetch=2,
            grid=(pairs,),
            in_specs=[column(0), column(1), column(2), whole_block(code_key.shape), whole_block(code_blk.shape)],
            out_specs=[column(0), pl.BlockSpec((1, blocks, LANES), lambda p, *_: (p, 0, 0))],
        ),
        out_shape=[
            jax.ShapeDtypeStruct((length, pairs * LANES), BF16),
            jax.ShapeDtypeStruct((pairs, blocks, LANES), F32),
        ],
        compiler_params=pltpu.CompilerParams(vmem_limit_bytes=VMEM_LIMIT),
    )(entry, most, project_low, project_low, project_low, code_key, code_blk)


def attend_backward(project_low, mixed, grad_mixed, lse, tables, scale, start, stop):
    entry, most, code_key, code_blk = tables
    length = project_low.shape[0]
    pairs = project_low.shape[1] // (3 * LANES)
    blocks = length // BLK
    shape = (length, 3 * (stop - start) * LANES)

    def column(kind):
        return pl.BlockSpec((length, LANES), lambda p, *_: (0, kind * pairs + p + start))

    return pl.pallas_call(
        partial(backward_kernel, scale=scale, start=start),
        grid_spec=pltpu.PrefetchScalarGridSpec(
            num_scalar_prefetch=2,
            grid=(stop - start,),
            in_specs=[
                column(0),
                column(1),
                column(2),
                column(0),
                column(0),
                pl.BlockSpec((1, blocks, LANES), lambda p, *_: (p + start, 0, 0)),
                whole_block(code_key.shape),
                whole_block(code_blk.shape),
            ],
            out_specs=whole_block(shape),
            scratch_shapes=[pltpu.VMEM((length, LANES), F32), pltpu.VMEM((length, LANES), F32)],
        ),
        out_shape=jax.ShapeDtypeStruct(shape, BF16),
        compiler_params=pltpu.CompilerParams(vmem_limit_bytes=VMEM_LIMIT),
    )(entry, most, project_low, project_low, project_low, mixed, grad_mixed, lse, code_key, code_blk)


class Weight:
    def __init__(self, own, layer, fetch, axis):
        self.axis, self.bit = axis, fetch.bit
        self.arrays = [own] + fetch.pieces
        rows, columns = own.shape[-2:]
        self.shape = (2 * rows, columns) if axis == 0 else (rows, 2 * columns)
        if own.ndim == 3:
            own_spec = pl.BlockSpec((1, rows, columns), lambda i: (layer, 0, 0))
        else:
            own_spec = whole_block(own.shape)
        self.specs = [own_spec] + [whole_block(piece.shape) for piece in fetch.pieces]

    def assemble(self, refs, place, into):
        own = refs[0]
        rows, columns = own.shape[-2:]
        into[0:rows, 0:columns] = own[0] if len(own.shape) == 3 else own[...]
        base = rows if self.axis == 0 else 0
        lanes = pl.ds(0 if self.axis == 0 else columns, columns)
        half = rows // 2
        into[pl.ds(pl.multiple_of(base + place * half, half), half), lanes] = refs[1][...]
        into[pl.ds(pl.multiple_of(base + (1 - place) * half, half), half), lanes] = refs[2][...]


def token_kernel(work, inputs, weights, outputs, place, length):
    block = min(TOKEN_BLOCK, length)
    in_specs, arrays = [pl.BlockSpec(memory_space=pltpu.SMEM)], [place]
    for item in inputs:
        if not isinstance(item, tuple):
            item = (ROWS, item, 0)
        array = item[1]
        if item[0] == WHOLE:
            in_specs.append(whole_block(array.shape))
        else:
            in_specs.append(pl.BlockSpec((block, array.shape[1]), lambda i, skip=item[2] // block: (i + skip, 0)))
        arrays.append(array)
    counts = []
    for weight in weights:
        in_specs += weight.specs
        arrays += weight.arrays
        counts.append(len(weight.arrays))
    out_specs, out_shapes = [], []
    for out in outputs:
        if out[0] == SUM:
            out_specs.append(whole_block(out[1:]))
            out_shapes.append(jax.ShapeDtypeStruct(out[1:], F32))
        else:
            out_specs.append(pl.BlockSpec((block, out[0]), lambda i: (i, 0)))
            out_shapes.append(jax.ShapeDtypeStruct((length, out[0]), out[1]))

    def kernel(*refs):
        place_ref, refs = refs[0], refs[1:]
        ins, refs = refs[: len(inputs)], refs[len(inputs) :]
        parts = []
        for count in counts:
            parts.append(refs[:count])
            refs = refs[count:]
        outs, scratch = refs[: len(outputs)], refs[len(outputs) :]
        step = pl.program_id(0)

        @pl.when(step == 0)
        def _():
            for weight, part, into in zip(weights, parts, scratch):
                weight.assemble(part, (place_ref[0, 0] >> weight.bit) & 1, into)
            for out, ref in zip(outputs, outs):
                if out[0] == SUM:
                    ref[...] = jnp.zeros_like(ref)

        work(ins, scratch, outs)

    return pl.pallas_call(
        kernel,
        grid=(length // block,),
        in_specs=in_specs,
        out_specs=out_specs,
        out_shape=out_shapes,
        scratch_shapes=[pltpu.VMEM(weight.shape, BF16) for weight in weights],
        compiler_params=pltpu.CompilerParams(vmem_limit_bytes=VMEM_LIMIT),
    )(*arrays)


def normed_of(value):
    mean = jnp.mean(value, axis=1, keepdims=True)
    centered = value - mean
    variance = jnp.mean(centered * centered, axis=1, keepdims=True)
    inverse = lax.rsqrt(variance + EPSILON)
    return centered * inverse, inverse


def norm_grad(grad_out, normed, inverse, gain):
    scaled = grad_out * gain
    mean = jnp.mean(scaled, axis=1, keepdims=True)
    along = jnp.mean(scaled * normed, axis=1, keepdims=True)
    return inverse * (scaled - mean - normed * along)


def add_rows(ref, *terms):
    for row, term in enumerate(terms):
        ref[row : row + 1, :] += jnp.sum(term, axis=0, keepdims=True)


def both(own_ref, got_ref):
    return own_ref[...].astype(F32) + got_ref[...].astype(F32)


def joined(refs):
    return jnp.concatenate([ref[...] for ref in refs], axis=1) if len(refs) > 1 else refs[0][...]


def put_halves(refs, value):
    half = value.shape[1] // 2
    refs[0][...] = value[:, :half].astype(refs[0].dtype)
    refs[1][...] = value[:, half:].astype(refs[1].dtype)


def project_kernel(ins, weights, outs):
    outs[0][...] = (dot_nn(joined(ins[:2]), weights[0][...]) + ins[2][...]).astype(BF16)


def norm_project_kernel(ins, weights, outs):
    own_ref, first_ref, got_ref, vec_ref, bias_ref = ins
    hidden_ref, low_own_ref, low_other_ref, hat_ref, inverse_ref, project_ref = outs
    normed, inverse = normed_of(first_ref[...] + (both(own_ref, got_ref) + vec_ref[0:1, :]))
    hidden = normed * vec_ref[1:2, :] + vec_ref[2:3, :]
    hidden_ref[...] = hidden
    low = hidden.astype(BF16)
    put_halves((low_own_ref, low_other_ref), low)
    hat_ref[...] = normed.astype(BF16)
    inverse_ref[...] = inverse
    project_ref[...] = (dot_nn(low, weights[0][...]) + bias_ref[...]).astype(BF16)


def product_kernel(ins, weights, outs):
    outs[0][...] = dot_nn(ins[0][...], weights[0][...]).astype(BF16)


def feed_forward_kernel(ins, weights, outs):
    own_ref, got_ref, vec_ref, bias_ref = ins[:4]
    first_ref, low_own_ref, low_other_ref, hat_ref, inverse_ref, active_ref, slope_ref, part_ref = outs
    hidden = joined(ins[4:]).astype(F32)
    normed, inverse = normed_of(hidden + (both(own_ref, got_ref) + vec_ref[0:1, :]))
    first = normed * vec_ref[1:2, :] + vec_ref[2:3, :]
    first_ref[...] = first
    low = first.astype(BF16)
    put_halves((low_own_ref, low_other_ref), low)
    hat_ref[...] = normed.astype(BF16)
    inverse_ref[...] = inverse
    inner = dot_nn(low, weights[0][...]) + bias_ref[...]
    square = inner * inner
    bent = jnp.tanh(GELU_SCALE * inner * (1.0 + GELU_CUBE * square))
    half = 0.5 * (1.0 + bent)
    active = (inner * half).astype(BF16)
    active_ref[...] = active
    slope = half + 0.5 * GELU_SCALE * inner * (1.0 - bent * bent) * (1.0 + 3.0 * GELU_CUBE * square)
    slope_ref[...] = slope.astype(BF16)
    part_ref[...] = dot_nn(active, weights[1][...]).astype(BF16)


def loss_kernel(ins, weights, outs):
    own_ref, first_ref, got_ref, vec_ref, goal_own_ref, goal_other_ref, live_ref = ins
    grad_ref, hidden_own_ref, hidden_other_ref, low_own_ref, low_other_ref, sums_ref, loss_ref = outs
    normed, inverse = normed_of(first_ref[...] + (both(own_ref, got_ref) + vec_ref[0:1, :]))
    hidden = normed * vec_ref[1:2, :] + vec_ref[2:3, :]
    put_halves((hidden_own_ref, hidden_other_ref), hidden)
    error = hidden - joined((goal_own_ref, goal_other_ref)).astype(F32)
    grad_out = live_ref[...] * error
    grad = norm_grad(grad_out, normed, inverse, vec_ref[1:2, :])
    grad_ref[...] = grad
    low = grad.astype(BF16)
    put_halves((low_own_ref, low_other_ref), low)
    add_rows(sums_ref, grad_out * normed, grad_out, low.astype(F32))
    squares = grad_out * error
    half = squares.shape[1] // 2
    add_rows(loss_ref, squares[:, :half] + squares[:, half:])


def second_norm_kernel(ins, weights, outs):
    own_ref, base_own_ref, base_other_ref, got_ref, hat_ref, inverse_ref, vec_ref = ins
    grad_ref, low_own_ref, low_other_ref, sums_ref = outs
    normed = hat_ref[...].astype(F32)
    grad_out = joined((base_own_ref, base_other_ref)) + both(own_ref, got_ref)
    grad = norm_grad(grad_out, normed, inverse_ref[...], vec_ref[1:2, :])
    grad_ref[...] = grad
    low = grad.astype(BF16)
    put_halves((low_own_ref, low_other_ref), low)
    add_rows(sums_ref, grad_out * normed, grad_out, low.astype(F32))


def feed_backward_kernel(ins, weights, outs):
    low_own_ref, low_other_ref, slope_ref = ins
    inner_ref, part_ref, sums_ref = outs
    low = joined((low_own_ref, low_other_ref))
    inner = (dot_nt(low, weights[0][...]) * slope_ref[...].astype(F32)).astype(BF16)
    inner_ref[...] = inner
    part_ref[...] = dot_nt(inner, weights[1][...]).astype(BF16)
    total = jnp.sum(inner.astype(F32), axis=0, keepdims=True)
    columns = sums_ref.shape[1]
    for row in range(total.shape[1] // columns):
        sums_ref[row : row + 1, :] += total[:, row * columns : (row + 1) * columns]


def first_norm_kernel(ins, weights, outs):
    own_ref, base_ref, got_ref, hat_ref, inverse_ref, vec_ref = ins
    grad_own_ref, grad_other_ref, low_own_ref, low_other_ref, mixed_ref, sums_ref = outs
    normed = hat_ref[...].astype(F32)
    grad_out = base_ref[...] + both(own_ref, got_ref)
    grad = norm_grad(grad_out, normed, inverse_ref[...], vec_ref[1:2, :])
    put_halves((grad_own_ref, grad_other_ref), grad)
    low = grad.astype(BF16)
    put_halves((low_own_ref, low_other_ref), low)
    mixed_ref[...] = dot_nt(low, weights[0][...]).astype(BF16)
    add_rows(sums_ref, grad_out * normed, grad_out, low.astype(F32))


def project_backward_kernel(cuts, ins, weights, outs):
    sums_ref = outs[-1]
    width = weights[0].shape[1] // 3
    part = None
    for ref, start, stop in zip(ins, cuts[:-1], cuts[1:]):
        lanes = (stop - start) * LANES
        sums_ref[0:1, start * LANES : stop * LANES] += jnp.sum(ref[:, 0:lanes].astype(F32), axis=0, keepdims=True)
        for kind in range(3):
            at = kind * width + start * LANES
            term = dot_nt(ref[:, kind * lanes : (kind + 1) * lanes], weights[0][:, at : at + lanes])
            part = term if part is None else part + term
    if len(outs) > 2:
        put_halves(outs, part)
    else:
        outs[0][...] = part.astype(BF16)


def pack_kernel(split_count, *refs):
    own_ref, other_ref = refs[-2:]
    half = own_ref.shape[1]
    for at, ref in enumerate(refs[:-2]):
        rows = slice(8 * at, 8 * at + 8)
        if at < split_count:
            own_ref[rows, :] = ref[:, :half]
            other_ref[rows, :] = ref[:, half:]
        else:
            own_ref[rows, :] = ref[...]
            other_ref[rows, :] = ref[...]


def pack(split_terms, whole_terms):
    half = whole_terms[0].shape[1]
    shape = jax.ShapeDtypeStruct((8 * (len(split_terms) + len(whole_terms)), half), F32)
    return pl.pallas_call(partial(pack_kernel, len(split_terms)), out_shape=[shape, shape])(
        *split_terms, *whole_terms
    )


def unpack_kernel(layers, rows_up, tokens, ref, *outs):
    half = ref.shape[1]
    scale_ref, loss_ref, split_refs, query_ref, up_ref = outs[0], outs[1], outs[2:8], outs[8], outs[9]
    base = 16 * layers
    count = ref[base + 16 * layers + 8 : base + 16 * layers + 9, 0:1]
    scale = 2.0 * tokens / count
    scale_ref[...] = jnp.broadcast_to(scale, scale_ref.shape)
    loss = jnp.sum(ref[base + 16 * layers : base + 16 * layers + 1, :], axis=1, keepdims=True)
    loss_ref[...] = jnp.broadcast_to(loss / (2.0 * half * count), loss_ref.shape)
    for layer in range(layers):
        at = slice(layer, layer + 1)
        for term in range(6):
            row = 16 * layer + 8 * (term // 3) + term % 3
            split_refs[term][at, :] = ref[row : row + 1, :] * scale
        row = base + 16 * layer
        query_ref[at, :] = ref[row : row + 1, :] * scale
        for part in range(rows_up):
            up_ref[at, part * half : (part + 1) * half] = ref[row + 8 + part : row + 9 + part, :] * scale


def unpack(terms, layers, feed, tokens):
    half = terms.shape[1]
    shapes = [(8, LANES), (8, LANES)] + [(layers, half)] * 7 + [(layers, feed)]
    return pl.pallas_call(
        partial(unpack_kernel, layers, feed // half, tokens),
        out_shape=[jax.ShapeDtypeStruct(shape, F32) for shape in shapes],
    )(terms)


def cross(block, pairs):
    return lax.ppermute(block, (ROW, COL), pairs)


class Sequence:
    def __init__(self, block):
        self.block = block
        self.sent = cross(block, [(0, 2), (3, 1)])
        self.got = cross(block, [(1, 0), (2, 3)])

    def pass_on(self, line):
        self.got = line.mark(line.next(self.got))
        self.sent = self.sent, cross(self.got, [(0, 2), (3, 1)])

    def halves(self):
        keeps = lax.axis_index(ROW) == lax.axis_index(COL)
        return [jnp.where(keeps, mine, sent) for mine, sent in zip((self.block, self.got), self.sent)]


def finish_kernel(layers, place_ref, scale_ref, *refs):
    step = pl.program_id(0)
    outs = refs[2 * layers :]
    scale = scale_ref[0:1, 0:1]
    for at in range(2 * layers):

        @pl.when(step == at)
        def _():
            value = refs[at][...].astype(F32) * scale
            start = 0
            for out in outs:
                columns = out.shape[-1]
                if len(out.shape) == 3:
                    out[0] = value[:, start : start + columns]
                    start += columns
                else:
                    for kind in range(out.shape[2]):
                        out[0, :, kind, :] = value[:, start : start + columns]
                        start += columns


def finish(halves, outputs, place, scale):
    layers = len(halves)
    arrays = [array for pair in halves for array in pair]
    rows = arrays[0].shape[0]

    def out_spec(shape):
        zeros = (0,) * len(shape)
        return pl.BlockSpec((1, rows) + shape, lambda i, place_ref: (i // 2, ((place_ref[0, 0] & 1) + i) % 2) + zeros)

    return pl.pallas_call(
        partial(finish_kernel, layers),
        grid_spec=pltpu.PrefetchScalarGridSpec(
            num_scalar_prefetch=1,
            grid=(2 * layers,),
            in_specs=[whole_block(scale.shape)] + [whole_block(array.shape) for array in arrays],
            out_specs=[out_spec(shape) for shape in outputs],
        ),
        out_shape=[jax.ShapeDtypeStruct((layers, 2 * rows) + shape, F32) for shape in outputs],
        compiler_params=pltpu.CompilerParams(vmem_limit_bytes=VMEM_LIMIT),
    )(place, scale, *arrays)


def body(
    tokens_in,
    teacher,
    qkv_weight,
    query_bias,
    out_weight,
    out_bias,
    first_gain,
    first_shift,
    up_weight,
    up_bias,
    down_weight,
    down_bias,
    second_gain,
    second_shift,
    random_blocks,
    segment_ids,
    padding_mask,
):
    row_count = lax.axis_size(ROW)
    layers, half, _, inner = qkv_weight.shape
    width = 2 * half
    feed = up_weight.shape[2]
    length = segment_ids.shape[1]
    heads_local = random_blocks.shape[1] // row_count
    head_width = inner // heads_local
    scale = head_width ** (-0.5)
    pairs = inner // LANES
    keeps = lax.axis_index(ROW) == lax.axis_index(COL)
    mine = lax.axis_index(COL)
    place = lax.axis_index(DP).astype(jnp.int32).reshape(1, 1)
    line = Line()

    stacks = {QKV: qkv_weight, OUT: out_weight, UP: up_weight, DOWN: down_weight}
    fetch, shard = {}, {}

    def ask(layer, name, bit):
        if layer < layers:
            fetch[layer, name] = Fetch(line, stacks[name], layer, bit)

    def pass_on(layer, name):
        if layer < layers:
            fetch[layer, name].pass_on(line)

    def arrived(layer, *names):
        if layer < layers:
            for name in names:
                pieces = fetch[layer, name].pieces
                pieces[1] = line.mark(line.next(pieces[1]))

    def weight(layer, name):
        own = shard[layer] if name == QKV else stacks[name]
        return Weight(own, layer, fetch[layer, name], 1 if name in (OUT, DOWN) else 0)

    def kernel(work, inputs, weights, outputs, main=0):
        first = inputs[0]
        first = (first[0], line.next(first[1])) + first[2:] if isinstance(first, tuple) else line.next(first)
        outs = token_kernel(work, [first] + inputs[1:], weights, outputs, place, length)
        line.mark(outs[main])
        return outs

    ask(0, QKV, 0)
    tokens = Sequence(tokens_in)
    vectors = jnp.stack([out_bias, first_gain, first_shift, down_bias, second_gain, second_shift])
    vectors = jnp.concatenate([vectors, swap(vectors, COL)], axis=2)
    shard[0] = line.mark(line.next(qkv_weight[0]).reshape(half, 3 * inner))
    pass_on(0, QKV)
    tokens.pass_on(line)
    ask(0, DOWN, 1)
    ask(0, OUT, 0)
    ask(0, UP, 0)
    segment = lax.dynamic_index_in_dim(segment_ids, mine, 0, keepdims=False)
    valid = lax.dynamic_index_in_dim(padding_mask, mine, 0, keepdims=False)
    local_blocks = lax.dynamic_slice_in_dim(random_blocks, lax.axis_index(ROW) * heads_local, heads_local, 1)
    tables = attention_tables(line.next(segment), valid, local_blocks, LANES // head_width)
    line.mark(vectors, *[part for table in tables for part in table])
    tokens_low = tokens.halves()

    saved = []
    for layer in range(layers):
        w = {QKV: weight(layer, QKV)}
        bias = jnp.concatenate([query_bias[layer], jnp.zeros((2 * inner,), F32)])[None]
        hidden_hat = hidden_inverse = None
        if layer == 0:
            hidden = hidden_low = tokens_low
            (project_low,) = kernel(
                project_kernel, hidden + [(WHOLE, bias)], [w[QKV]], [(3 * inner, BF16)]
            )
            pass_on(0, DOWN)
            pass_on(0, OUT)
            pass_on(0, UP)
            ask(1, QKV, 0)
            ask(1, OUT, 1)
        else:
            hidden, low_own, low_other, hidden_hat, hidden_inverse, project_low = kernel(
                norm_project_kernel,
                [part, first, got, (WHOLE, saved[-1].second_vec), (WHOLE, bias)],
                [w[QKV]],
                [(width, F32), (half, BF16), (half, BF16), (width, BF16), (1, F32), (3 * inner, BF16)],
                main=5,
            )
            hidden, hidden_low = [hidden], (low_own, low_other)
            if layer == 1:
                pass_on(layer, DOWN)
            if layer == layers - 1:
                goal = Sequence(line.next(teacher))
        first_vec, second_vec = vectors[0:3, layer], vectors[3:6, layer]
        mixed, lse = attend_forward(line.next(project_low), tables[layer], scale)
        line.mark(mixed)
        arrived(layer, OUT, UP, DOWN)
        if layer == 0:
            pass_on(1, QKV)
            pass_on(1, OUT)
        if layer == layers - 1:
            goal.pass_on(line)
        w[OUT] = weight(layer, OUT)
        (part,) = kernel(product_kernel, [mixed], [w[OUT]], [(width, BF16)])
        got = swap(part, ROW)
        if layer == 0:
            ask(1, UP, 0)
            ask(1, DOWN, 1)
        w[UP], w[DOWN] = weight(layer, UP), weight(layer, DOWN)
        first, first_own, first_other, first_hat, first_inverse, active, slope, part = kernel(
            feed_forward_kernel,
            [part, got, (WHOLE, first_vec), (WHOLE, up_bias[layer][None])] + hidden,
            [w[UP], w[DOWN]],
            [(width, F32), (half, BF16), (half, BF16), (width, BF16), (1, F32), (feed, BF16), (feed, BF16), (width, BF16)],
            main=7,
        )
        got = swap(part, ROW)
        if layer == 0:
            arrived(1, QKV, OUT)
            pass_on(1, UP)
            if layers > 1:
                shard[1] = line.mark(line.next(qkv_weight[1]).reshape(half, 3 * inner))
        saved.append(
            SimpleNamespace(
                w=w,
                first_vec=first_vec,
                second_vec=second_vec,
                hidden_low=hidden_low,
                hidden_hat=hidden_hat,
                hidden_inverse=hidden_inverse,
                project_low=project_low,
                mixed=mixed,
                lse=lse,
                first_low=(first_own, first_other),
                first_hat=first_hat,
                first_inverse=first_inverse,
                active=active,
                slope=slope,
            )
        )

    live = valid.astype(F32)[:, None]
    goal = goal.halves()

    chains = {}

    def steps(*keys):
        for key in keys:
            if key in chains:
                chains[key].step(line)

    def matmul(left, right):
        return line.mark(dot_tn(left, line.next(right)))

    def matmul_low(left, right):
        return line.mark(lax.optimization_barrier(dot_tn(left, line.next(right))).astype(BF16))

    split_terms, whole_terms = [None] * (2 * layers), [None] * (2 * layers)
    for layer in reversed(range(layers)):
        final, above = layer == 0, layer + 1
        keep = saved[layer]
        w = keep.w
        if layer == layers - 1:
            grad_second, hidden_own, hidden_other, low_own, low_other, second_sums, loss_sums = kernel(
                loss_kernel,
                [part, first, got, (WHOLE, keep.second_vec), *goal, live],
                [],
                [(width, F32), (half, F32), (half, BF16), (half, BF16), (half, BF16), (SUM, 8, width), (SUM, 8, half)],
                main=4,
            )
        else:
            grad_second, low_own, low_other, second_sums = kernel(
                second_norm_kernel,
                [part, *grad_hidden, got, saved[above].hidden_hat, saved[above].hidden_inverse, (WHOLE, keep.second_vec)],
                [],
                [(width, F32), (half, BF16), (half, BF16), (SUM, 8, width)],
                main=2,
            )
        chains[layer, DOWN] = Reduce(matmul_low(keep.active, low_other), final)
        steps((above, DOWN), (above, UP), (above, OUT_QKV))
        grad_inner, part, up_sums = kernel(
            feed_backward_kernel,
            [low_own, low_other, keep.slope],
            [w[DOWN], w[UP]],
            [(feed, BF16), (width, BF16), (SUM, 8, half)],
            main=1,
        )
        got = swap(part, ROW)
        first_own, first_other = keep.first_low
        chains[layer, UP] = Reduce(matmul_low(first_other, grad_inner), final)
        chains[layer, UP].own = matmul(first_own, grad_inner)
        chains[layer, DOWN].own = matmul(keep.active, low_own)
        steps((above, DOWN), (above, UP))
        *grad_hidden, low_own, low_other, grad_mixed, first_sums = kernel(
            first_norm_kernel,
            [part, grad_second, got, keep.first_hat, keep.first_inverse, (WHOLE, keep.first_vec)],
            [w[OUT]],
            [(half, F32), (half, F32), (half, BF16), (half, BF16), (inner, BF16), (SUM, 8, width)],
            main=4,
        )
        out_other = matmul_low(keep.mixed, low_other)
        out_own = matmul(keep.mixed, low_own)
        if final:
            cuts = [0, pairs - 1, pairs] if pairs > 1 else [0, pairs]
            steps((above, OUT_QKV), (layer, DOWN))
        else:
            cuts = [0, pairs]
            steps((layer, DOWN))
        input_own, input_other = keep.hidden_low
        projects = []
        for start, stop in zip(cuts[:-1], cuts[1:]):
            grad_project = attend_backward(
                keep.project_low, keep.mixed, line.next(grad_mixed), keep.lse, tables[layer], scale, start, stop
            )
            line.mark(grad_project)
            projects.append(grad_project)
            qkv_other = matmul_low(input_other, grad_project)
            if start == 0:
                qkv_other = line.mark(jnp.concatenate([out_other, qkv_other], axis=1))
            name = OUT_QKV if start == 0 else QKV_REST
            chains[layer, name] = Reduce(qkv_other, final and start == 0)
            if not final:
                steps((layer, DOWN), (layer, UP))
            if final:
                if stop < pairs:
                    steps((above, DOWN), (above, UP), (above, OUT_QKV), (layer, DOWN), (layer, UP))
                qkv_own = matmul(input_own, grad_project)
                chains[layer, name].own = jnp.concatenate([out_own, qkv_own], axis=1) if start == 0 else qkv_own
        outputs = [(half, BF16), (half, BF16)] if final else [(width, BF16)]

        def project_backward():
            return kernel(
                partial(project_backward_kernel, cuts),
                projects,
                [w[QKV]],
                outputs + [(SUM, 8, inner)],
            )

        if not final:
            part, query_sums = project_backward()
            got = swap(part, ROW)
            qkv_own = matmul(input_own, grad_project)
            chains[layer, name].own = jnp.concatenate([out_own, qkv_own], axis=1)
            whole_terms[2 * layer] = query_sums
        split_terms[2 * layer : 2 * layer + 2] = [second_sums, first_sums]
        whole_terms[2 * layer + 1] = up_sums

    def tail(*names):
        for name in names:
            chain = chains[name]
            if chain.done():
                chain.collect(line)
            else:
                chain.step(line)

    def send_terms(terms, got, turn):
        terms = line.mark(terms + line.next(got))
        return terms, swap_bit(terms, turn) if turn < dp_bits() else None

    tail((1, UP), (0, DOWN), (0, UP), (1, OUT_QKV))
    part_own, part_other, whole_terms[0] = project_backward()
    got = swap(jnp.where(keeps, part_other, part_own), ROW)
    count = jnp.sum(padding_mask.astype(F32)) * jnp.full((8, half), 0.5, F32)
    own, other = pack(split_terms, whole_terms + [loss_sums, count])
    terms, terms_got = line.mark(own), swap(other, COL)
    tail((0, OUT_QKV), (0, DOWN), (0, UP), (0, QKV_REST))
    got = line.next(got).astype(F32)
    grad = jnp.where(keeps, grad_hidden[0] + part_own.astype(F32), grad_hidden[1] + part_other.astype(F32)) + got
    grad_got = cross(line.mark(grad.astype(BF16)), [(1, 2), (2, 1)])
    terms, terms_got = send_terms(terms, terms_got, 0)
    tail((0, OUT_QKV), (0, DOWN), (0, UP), (0, QKV_REST))
    terms, terms_got = send_terms(terms, terms_got, 1)
    crossed = cross(line.next(hidden_other), [(0, 1), (3, 2)])
    tail((0, DOWN), (0, OUT_QKV), (0, UP), (0, QKV_REST))
    turn = 2
    while turn <= dp_bits():
        terms, terms_got = send_terms(terms, terms_got, turn)
        turn += 1
    tail((0, OUT_QKV), (0, UP), (0, QKV_REST))
    while not all(chain.done() for chain in chains.values()):
        steps(*chains)
    scale_block, loss, *vectors = unpack(terms, layers, feed, float(length * row_count * lax.axis_size(DP)))
    loss = loss[0, 0]
    hidden_out = jnp.where(keeps, hidden_own, crossed.astype(F32))
    input_grad = jnp.where(keeps, grad, grad_got.astype(F32)) * scale_block[0:1, 0:1]

    def halves_of(name):
        return [chains[i, name].halves() for i in range(layers)]

    (down_grads,) = finish(halves_of(DOWN), [(half,)], place, scale_block)
    (up_grads,) = finish(halves_of(UP), [(feed,)], place, scale_block)
    halves = []
    for layer in range(layers):
        pair = []
        for side in range(2):
            value = chains[layer, OUT_QKV].halves()[side]
            if (layer, QKV_REST) in chains:
                more = chains[layer, QKV_REST].halves()[side]
                rows = value.shape[0]
                kinds = [value[:, half:].reshape(rows, 3, -1), more.reshape(rows, 3, -1)]
                kinds = jnp.concatenate(kinds, axis=2).reshape(rows, 3 * inner)
                value = jnp.concatenate([value[:, :half], kinds], axis=1)
            pair.append(value)
        halves.append(tuple(pair))
    out_grads, query_key_grads, value_grads = finish(
        halves, [(half,), (2, inner), (inner,)], place, scale_block
    )
    second_gain_grad, second_shift_grad, down_bias_grad, first_gain_grad, first_shift_grad, out_bias_grad = vectors[:6]
    return (
        hidden_out,
        loss,
        input_grad,
        query_key_grads,
        value_grads,
        vectors[6],
        out_grads,
        out_bias_grad,
        first_gain_grad,
        first_shift_grad,
        up_grads,
        vectors[7],
        down_grads,
        down_bias_grad,
        second_gain_grad,
        second_shift_grad,
    )


def solution(mesh):
    return jax.shard_map(
        body,
        mesh=mesh,
        in_specs=(
            P((DP, ROW), COL),
            P((DP, ROW), COL),
            P(None, COL, None, ROW),
            P(None, ROW),
            P(None, ROW, COL),
            P(None, COL),
            P(None, COL),
            P(None, COL),
            P(None, COL, ROW),
            P(None, ROW),
            P(None, ROW, COL),
            P(None, COL),
            P(None, COL),
            P(None, COL),
            P(),
            P(DP, None),
            P(DP, None),
        ),
        out_specs=(
            P((DP, ROW), COL),
            P(),
            P((DP, ROW), COL),
            P(None, COL, None, ROW),
            P(None, COL, ROW),
            P(None, ROW),
            P(None, ROW, COL),
            P(None, COL),
            P(None, COL),
            P(None, COL),
            P(None, COL, ROW),
            P(None, ROW),
            P(None, ROW, COL),
            P(None, COL),
            P(None, COL),
            P(None, COL),
        ),
        check_vma=False,
    )
```

time: 3020 us -> 573 us (0.19)
  waiting for transfers between devices: 1310 us -> 105 us
  local copies, waits for them, and re-layouts: 978 us -> 79.1 us
  matrix products: 382 us -> 39 us
  Pallas kernels: 0 us -> 191 us
  blocking collectives: 183 us -> 0 us
  starting transfers between devices: 3.34 us -> 88.5 us
  other arithmetic: 130 us -> 58.5 us
    gather x13 -> x0, local copies, waits for them, and re-layouts: 733 us -> none  [the longest x8 367 us: allowed_pairs(): same = segment[query_pos][..., :, None] == segment[key_pos][..., None, :]]
    all_gather x16 -> x0, waiting for transfers between devices: 560 us -> none  [the longest x4 261 us: backward_rows(): grad_all = lax.all_gather(grad_low, 'col', axis=0, tiled=True)]
    reduce_scatter x16 -> x0, waiting for transfers between devices: 426 us -> none  [the longest x4 210 us: backward_cols(): lax.psum_scatter(term(jnp.int32(0), grad_low.shape[0] * lax.axis_size('co...]
    dot_general x56 -> x18, matrix products: 382 us -> 39 us  [dot_tn(): lax.dot_general(left, right, (((0,), (0,)), ((), ())), preferred_element_...]
    psum x1 -> x0, waiting for transfers between devices: 324 us -> none  [body(): lax.psum((stacked[0], stacked[1], stacked[2], stacked[3], stacked[4], sta...]
    pallas_call x0 -> x24, Pallas kernels: none -> 191 us  [the longest x14 98.5 us: token_kernel(): pl.pallas_call(kernel, grid=(length // block,), in_specs=in_specs, out_sp...]
    psum x11 -> x0, blocking collectives: 183 us -> none  [the longest x1 65.5 us: body(): gains = lax.psum((gains[0], gains[1], gains[2], gains[3]), ('dp', 'row'))]
    reshape x18 -> x8, local copies, waits for them, and re-layouts: 155 us -> 5.19 us  [the longest x1 2.27 us: body(): shard[1] = line.mark(line.next(qkv_weight[1]).reshape(half, 3 * inner))]
  transfers between devices with their start and end apart: 33 -> 75, of which waited for: 30 -> 20; matrix products, arithmetic and copies ran while one was open for 27% -> 25% of each run, Pallas kernels for 0% -> 24%
where the time goes in v1:
time: 573 us; the launch traced here: 565 us
  Pallas kernels  191 us (33%)
  waiting for transfers between devices  105 us (18%)
  starting transfers between devices  88.5 us (15%)
  local copies, waits for them, and re-layouts  79.1 us (14%)
  other arithmetic  58.5 us (10%)
  matrix products  39 us (7%)
    pallas_call x14, Pallas kernels, token_kernel(): pl.pallas_call(kernel, grid=(length // block,), in_specs=in_specs, out_sp...  98.5 us
    ppermute x42, waiting for transfers between devices, swap_bit(): return lax.ppermute(value, DP, [(i, i ^ 1 << bit) for i in range(count)])  64.7 us
    pallas_call x3, Pallas kernels, attend_backward(): pl.pallas_call(partial(backward_kernel, scale=scale, start=start), grid_s...  52.6 us
    ppermute x42, starting transfers between devices, swap_bit(): return lax.ppermute(value, DP, [(i, i ^ 1 << bit) for i in range(count)])  47.2 us
    ppermute x25, waiting for transfers between devices, swap(): return lax.ppermute(value, axis, [(0, 1), (1, 0)])  40.8 us
    unnamed x280, local copies, waits for them, and re-layouts  39.1 us
    dot_general x18, matrix products, dot_tn(): lax.dot_general(left, right, (((0,), (0,)), ((), ())), preferred_element_...  39 us
    convert_element_type x26, other arithmetic, step(): self.sent = sum((part.astype(F32) for part in parts)).astype(BF16)  28.9 us
  transfers between devices with their start and end apart: 75, of which 20 were waited for; matrix products, arithmetic and copies ran while one was open for 25% of the time, Pallas kernels for 24%

profile of v1, /device:TPU:0, one launch (start us, length us, event | category | flops | bytes accessed | tf_op | source)
XLA Modules:
  0.0 565.1 jit_solution(206001022093208216)
XLA Ops:
  2.0 6.8 %collective-permute-start.2 = (bf16[1024,384]{1,0:T(8,128)(2,1)}, bf16[1024,384]{1,0:T(8,128)(2,1)}, u32[]{:S(2)}, u32[]{:S(2)}) collective-permute-start(bf16[1024,384]{1,0:T(8,128)(2,1)} %param.18), channel_id=1, source_target_pairs={{0,2},{3,1},{4,6},{7,5},{8,10},{11,9},{12,14},{15,13},{16,18},{19,... | collective-permute-start | bytes 2359304 | tf_op jit(solution)/shard_map/ppermute | solution.py:678
  20.1 4.5 collective-permute-done.1.refs_5_.refs_4_
  57.4 11.3 %collective-permute-done.6.refs_8_ = bf16[192,1536]{1,0:T(8,128)(2,1)} collective-permute-done((bf16[192,1536]{1,0:T(8,128)(2,1)}, bf16[192,1536]{1,0:T(8,128)(2,1)}, u32[]{:S(2)}, u32[]{:S(2)}) %collective-permute-start.6) | collective-permute-done | bytes 589856 | tf_op jit(solution)/shard_map/ppermute | solution.py:33
  77.4 13.3 %shard_map.298 = (bf16[1024,384]{1,0:T(8,128)(2,1)S(1)}, f32[3,16,128]{2,1,0:T(8,128)S(1)}) custom-call(s32[3,14,11]{2,1,0:T(8,128)S(1)} %bitcast.186, s32[3]{0:T(128)S(1)} %get-tuple-element.410.most_ref, bf16[1024,1152]{1,0:T(8,128)(2,1)S(1)} %shard_map.297.q_ref.k_ref.v_ref, bf16[1024,1152]{1,0:T(8,128)(2,1)S(1)} %shard_map.297.q_ref.k_ref.v_ref, ...), custom_call_target="tpu_custom_call" | custom-call | tf_op jit(solution)/shard_map/pallas_call | solution.py:348
  109.6 13.1 %shard_map.300 = (f32[1024,768]{1,0:T(8,128)}, bf16[1024,384]{1,0:T(8,128)(2,1)S(1)}, bf16[1024,384]{1,0:T(8,128)(2,1)S(1)}, bf16[1024,768]{1,0:T(8,128)(2,1)}, ...) custom-call(s32[1,1]{1,0:T(1,128)} %bitcast.refs_0_.place_ref, ...), custom_call_target="tpu_custom_call" | custom-call | tf_op jit(solution)/shard_map/pallas_call | solution.py:466
  132.0 7.7 %collective-permute-done.17.refs_8_.refs_4_ = bf16[192,1152]{1,0:T(8,128)(2,1)} collective-permute-done((bf16[192,1152]{1,0:T(8,128)(2,1)}, bf16[192,1152]{1,0:T(8,128)(2,1)}, u32[]{:S(2)}, u32[]{:S(2)}) %collective-permute-start.17) | collective-permute-done | bytes 442400 | tf_op jit(solution)/shard_map/ppermute | solution.py:38
  146.6 7.6 %shard_map.301 = (f32[1024,768]{1,0:T(8,128)}, bf16[1024,384]{1,0:T(8,128)(2,1)S(1)}, bf16[1024,384]{1,0:T(8,128)(2,1)S(1)}, bf16[1024,768]{1,0:T(8,128)(2,1)S(1...) custom-call(s32[1,1]{1,0:T(1,128)} %bitcast.refs_0_.place_ref, bf16[1024,768]{1,0:T(8,128)(2,1)} %get-tuple-element.226.refs_1_, ...), custom_call_target="tpu_custom_call" | custom-call | tf_op jit(solution)/shard_map/pallas_call | solution.py:466
  162.1 13.7 %shard_map.302 = (bf16[1024,384]{1,0:T(8,128)(2,1)S(1)}, f32[3,16,128]{2,1,0:T(8,128)S(1)}) custom-call(s32[3,14,11]{2,1,0:T(8,128)S(1)} %bitcast.189, s32[3]{0:T(128)S(1)} %copy-done.83, bf16[1024,1152]{1,0:T(8,128)(2,1)S(1)} %copy-done.2, bf16[1024,1152]{1,0:T(8,128)(2,1)S(1)} %copy-done.2, bf16[1024,1152]{1,0:T(8,128)(2,1)S(1)} %copy-done.2, ...), custom_call_target="tpu_custom_call" | custom-call | tf_op jit(solution)/shard_map/pallas_call | solution.py:348
  184.4 12.7 %shard_map.304 = (f32[1024,768]{1,0:T(8,128)}, bf16[1024,384]{1,0:T(8,128)(2,1)S(1)}, bf16[1024,384]{1,0:T(8,128)(2,1)S(1)}, bf16[1024,768]{1,0:T(8,128)(2,1)S(1...) custom-call(s32[1,1]{1,0:T(1,128)} %bitcast.refs_0_.place_ref, ...), custom_call_target="tpu_custom_call" | custom-call | tf_op jit(solution)/shard_map/pallas_call | solution.py:466
  211.4 7.3 %shard_map.305 = (f32[1024,768]{1,0:T(8,128)}, f32[1024,384]{1,0:T(8,128)S(1)}, bf16[1024,384]{1,0:T(8,128)(2,1)}, bf16[1024,384]{1,0:T(8,128)(2,1)S(1)}, bf16[1...) custom-call(s32[1,1]{1,0:T(1,128)} %bitcast.refs_0_.place_ref, ...), custom_call_target="tpu_custom_call" | custom-call | tf_op jit(solution)/shard_map/pallas_call | solution.py:466
  221.7 9.6 %shard_map.306 = (bf16[1024,1536]{1,0:T(8,128)(2,1)}, bf16[1024,768]{1,0:T(8,128)(2,1)}, f32[8,384]{1,0:T(8,128)S(1)}) custom-call(s32[1,1]{1,0:T(1,128)} %bitcast.refs_0_.place_ref, bf16[1024,384]{1,0:T(8,128)(2,1)S(1)} %get-tuple-element.257.refs_1_, bf16[1024,384]{1,0:T(8,128)(2,1)S(1)} %get-tuple-element.248.refs_2_, ...), custom_call_target="tpu_custom_call" | custom-call | tf_op jit(solution)/shard_map/pallas_call | solution.py:466
  235.3 4.7 fusion.35
  244.0 6.7 %shard_map.307 = (f32[1024,384]{1,0:T(8,128)S(1)}, f32[1024,384]{1,0:T(8,128)}, bf16[1024,384]{1,0:T(8,128)(2,1)S(1)}, bf16[1024,384]{1,0:T(8,128)(2,1)S(1)}, bf...) custom-call(s32[1,1]{1,0:T(1,128)} %bitcast.refs_0_.place_ref, bf16[1024,768]{1,0:T(8,128)(2,1)} %get-tuple-element.258.refs_1_, ...), custom_call_target="tpu_custom_call" | custom-call | tf_op jit(solution)/shard_map/pallas_call | solution.py:466
  252.8 9.5 %collective-permute-done.28 = bf16[1536,384]{1,0:T(8,128)(2,1)S(1)} collective-permute-done((bf16[1536,384]{1,0:T(8,128)(2,1)}, bf16[1536,384]{1,0:T(8,128)(2,1)S(1)}, u32[]{:S(2)}, u32[]{:S(2)}) %collective-permute-start.28) | collective-permute-done | bytes 1179680 | tf_op jit(solution)/shard_map/ppermute | solution.py:33
  264.6 25.9 %shard_map.308.refs_1_ = bf16[1024,1152]{1,0:T(8,128)(2,1)S(1)} custom-call(s32[3,14,11]{2,1,0:T(8,128)S(1)} %bitcast.190, s32[3]{0:T(128)S(1)} %copy-done.84, bf16[1024,1152]{1,0:T(8,128)(2,1)} %get-tuple-element.230.q_ref.k_ref.v_ref, bf16[1024,1152]{1,0:T(8,128)(2,1)} %get-tuple-element.230.q_ref.k_ref.v_ref, ...), custom_call_target="tpu_custom_call" | custom-call | tf_op jit(solution)/shard_map/pallas_call | solution.py:374
  296.8 5.2 shard_map.309
  315.7 6.4 %shard_map.310 = (f32[1024,768]{1,0:T(8,128)}, bf16[1024,384]{1,0:T(8,128)(2,1)S(1)}, bf16[1024,384]{1,0:T(8,128)(2,1)S(1)}, f32[8,768]{1,0:T(8,128)S(1)}) custom-call(s32[1,1]{1,0:T(1,128)} %bitcast.refs_0_.place_ref, bf16[1024,768]{1,0:T(8,128)(2,1)} %get-tuple-element.278.refs_1_, f32[1024,384]{1,0:T(8,128)S(1)} %copy-done.36, ...), custom_call_target="tpu_custom_call" | custom-call | tf_op jit(solution)/shard_map/pallas_call | solution.py:466
  322.1 4.9 fusion.42
  327.2 9.5 %collective-permute-start.36 = (bf16[768,384]{1,0:T(8,128)(2,1)S(1)}, bf16[768,384]{1,0:T(8,128)(2,1)}, u32[]{:S(2)}, u32[]{:S(2)}) collective-permute-start(bf16[768,384]{1,0:T(8,128)(2,1)S(1)} %add_convert_fusion.8), channel_id=1, source_target_pairs={{0,16},{4,20},{8,24},{12,28},{16,0},{20,4},{24,8},{28,12},{1,17},{... | collective-permute-start | bytes 1769480 | tf_op jit(solution)/shard_map/ppermute | solution.py:38
  338.4 9.7 %shard_map.311 = (bf16[1024,1536]{1,0:T(8,128)(2,1)}, bf16[1024,768]{1,0:T(8,128)(2,1)S(1)}, f32[8,384]{1,0:T(8,128)S(1)}) custom-call(s32[1,1]{1,0:T(1,128)} %bitcast.refs_0_.place_ref, bf16[1024,384]{1,0:T(8,128)(2,1)S(1)} %get-tuple-element.299.refs_1_, bf16[1024,384]{1,0:T(8,128)(2,1)S(1)} %get-tuple-element.287.refs_2_, ...), custom_call_target="tpu_custom_call" | custom-call | tf_op jit(solution)/shard_map/pallas_call | solution.py:466
  348.2 4.8 fusion.43
  357.9 4.6 collective-permute-done.36
  369.4 6.6 %shard_map.312 = (f32[1024,384]{1,0:T(8,128)S(1)}, f32[1024,384]{1,0:T(8,128)}, bf16[1024,384]{1,0:T(8,128)(2,1)S(1)}, bf16[1024,384]{1,0:T(8,128)(2,1)S(1)}, bf...) custom-call(s32[1,1]{1,0:T(1,128)} %bitcast.refs_0_.place_ref, bf16[1024,768]{1,0:T(8,128)(2,1)} %copy-done.38, ...), custom_call_target="tpu_custom_call" | custom-call | tf_op jit(solution)/shard_map/pallas_call | solution.py:466
  392.9 17.5 %shard_map.313.refs_1_ = bf16[1024,768]{1,0:T(8,128)(2,1)S(1)} custom-call(s32[3,14,11]{2,1,0:T(8,128)S(1)} %bitcast.187, s32[3]{0:T(128)S(1)} %get-tuple-element.410.most_ref, bf16[1024,1152]{1,0:T(8,128)(2,1)S(1)} %shard_map.297.q_ref.k_ref.v_ref, bf16[1024,1152]{1,0:T(8,128)(2,1)S(1)} %shard_map.297.q_ref.k_ref.v_ref, ...), custom_call_target="tpu_custom_call" | custom-call | tf_op jit(solution)/shard_map/pallas_call | solution.py:374
  424.6 9.1 %shard_map.314.refs_2_ = bf16[1024,384]{1,0:T(8,128)(2,1)S(1)} custom-call(s32[3,14,11]{2,1,0:T(8,128)S(1)} %bitcast.188, s32[3]{0:T(128)S(1)} %get-tuple-element.410.most_ref, bf16[1024,1152]{1,0:T(8,128)(2,1)S(1)} %shard_map.297.q_ref.k_ref.v_ref, bf16[1024,1152]{1,0:T(8,128)(2,1)S(1)} %shard_map.297.q_ref.k_ref.v_ref, ...), custom_call_target="tpu_custom_call" | custom-call | tf_op jit(solution)/shard_map/pallas_call | solution.py:374
  445.6 12.6 %collective-permute-done.42 = bf16[192,1536]{1,0:T(8,128)(2,1)S(1)} collective-permute-done((bf16[192,1536]{1,0:T(8,128)(2,1)S(1)}, bf16[192,1536]{1,0:T(8,128)(2,1)S(1)}, u32[]{:S(2)}, u32[]{:S(2)}) %collective-permute-start.42) | collective-permute-done | bytes 589856 | tf_op jit(solution)/shard_map/ppermute | solution.py:38
  482.7 8.3 %collective-permute-done.56 = bf16[96,1536]{1,0:T(8,128)(2,1)S(1)} collective-permute-done((bf16[96,1536]{1,0:T(8,128)(2,1)S(1)}, bf16[96,1536]{1,0:T(8,128)(2,1)S(1)}, u32[]{:S(2)}, u32[]{:S(2)}) %collective-permute-start.56) | collective-permute-done | bytes 294944 | tf_op jit(solution)/shard_map/ppermute | solution.py:38
  495.0 10.2 %collective-permute-done.64.refs_1_ = bf16[768,384]{1,0:T(8,128)(2,1)S(1)} collective-permute-done((bf16[768,384]{1,0:T(8,128)(2,1)S(1)}, bf16[768,384]{1,0:T(8,128)(2,1)S(1)}, u32[]{:S(2)}, u32[]{:S(2)}) %collective-permute-start.64) | collective-permute-done | bytes 589856 | tf_op jit(solution)/shard_map/ppermute | solution.py:38
  512.7 4.9 collective-permute-start.59
  527.1 4.1 shard_map.320
  541.0 4.5 collective-permute-done.68
  553.5 6.2 %collective-permute-done.72 = bf16[192,384]{1,0:T(8,128)(2,1)} collective-permute-done((bf16[192,384]{1,0:T(8,128)(2,1)S(1)}, bf16[192,384]{1,0:T(8,128)(2,1)}, u32[]{:S(2)}, u32[]{:S(2)}) %collective-permute-start.72) | collective-permute-done | bytes 147488 | tf_op jit(solution)/shard_map/ppermute | solution.py:38
  (581 shorter events, 277.9 us)
Async XLA Ops:
  0.7 26.5 %collective-permute-start = (bf16[1024,384]{1,0:T(8,128)(2,1)}, bf16[1024,384]{1,0:T(8,128)(2,1)}, u32[]{:S(2)}, u32[]{:S(2)}) collective-permute-start(bf16[1024,384]{1,0:T(8,128)(2,1)} %param.18), channel_id=1, source_target_pairs={{1,0},{2,3},{5,4},{6,7},{9,8},{10,11},{13,12},{14,15},{17,16},{18,... | collective-permute-start | bytes 2359304 | tf_op jit(solution)/shard_map/ppermute | solution.py:678
  2.0 38.6 %collective-permute-start.2 = (bf16[1024,384]{1,0:T(8,128)(2,1)}, bf16[1024,384]{1,0:T(8,128)(2,1)}, u32[]{:S(2)}, u32[]{:S(2)}) collective-permute-start(bf16[1024,384]{1,0:T(8,128)(2,1)} %param.18), channel_id=1, source_target_pairs={{0,2},{3,1},{4,6},{7,5},{8,10},{11,9},{12,14},{15,13},{16,18},{19,... | collective-permute-start | bytes 2359304 | tf_op jit(solution)/shard_map/ppermute | solution.py:678
  24.6 20.0 %collective-permute-start.5 = (bf16[192,1152]{1,0:T(8,128)(2,1)S(1)}, bf16[192,1152]{1,0:T(8,128)(2,1)S(1)}, u32[]{:S(2)}, u32[]{:S(2)}) collective-permute-start(bf16[192,1152]{1,0:T(8,128)(2,1)S(1)} %collective-permute-done.1.refs_5_.refs_4_), channel_id=1, source_target_pairs={{0,4},{4,0},{8,12},{12,8},{16,20},{20,16},{24,28},{28,24},{1,5},{5... | collective-permute-start | bytes 1327112 | tf_op jit(solution)/shard_map/ppermute | solution.py:38
  40.5 28.2 %collective-permute-start.6 = (bf16[192,1536]{1,0:T(8,128)(2,1)}, bf16[192,1536]{1,0:T(8,128)(2,1)}, u32[]{:S(2)}, u32[]{:S(2)}) collective-permute-start(bf16[192,1536]{1,0:T(8,128)(2,1)} %dynamic-slice_bitcast_fusion.2), channel_id=1, source_target_pairs={{0,1},{1,0},{2,3},{3,2},{4,5},{5,4},{6,7},{7,6},{8,9},{9,8},{10,11... | collective-permute-start | bytes 1769480 | tf_op jit(solution)/shard_map/ppermute | solution.py:33
  68.7 22.6 %collective-permute-start.12 = (bf16[192,1536]{1,0:T(8,128)(2,1)}, bf16[192,1536]{1,0:T(8,128)(2,1)}, u32[]{:S(2)}, u32[]{:S(2)}) collective-permute-start(bf16[192,1536]{1,0:T(8,128)(2,1)} %collective-permute-done.6.refs_8_), channel_id=1, source_target_pairs={{0,4},{4,0},{8,12},{12,8},{16,20},{20,16},{24,28},{28,24},{1,5},{5... | collective-permute-start | bytes 1769480 | tf_op jit(solution)/shard_map/ppermute | solution.py:38
  69.3 22.0 %collective-permute-start.11 = (bf16[768,384]{1,0:T(8,128)(2,1)}, bf16[768,384]{1,0:T(8,128)(2,1)}, u32[]{:S(2)}, u32[]{:S(2)}) collective-permute-start(bf16[768,384]{1,0:T(8,128)(2,1)} %collective-permute-done.8.refs_11_.refs_5_), channel_id=1, source_target_pairs={{0,8},{4,12},{8,0},{12,4},{16,24},{20,28},{24,16},{28,20},{1,9},{5... | collective-permute-start | bytes 1769480 | tf_op jit(solution)/shard_map/ppermute | solution.py:38
  126.2 31.9 %collective-permute-start.19 = (bf16[768,384]{1,0:T(8,128)(2,1)}, bf16[768,384]{1,0:T(8,128)(2,1)}, u32[]{:S(2)}, u32[]{:S(2)}) collective-permute-start(bf16[768,384]{1,0:T(8,128)(2,1)} %dynamic-slice_bitcast_fusion), channel_id=1, source_target_pairs={{0,1},{1,0},{2,3},{3,2},{4,5},{5,4},{6,7},{7,6},{8,9},{9,8},{10,11... | collective-permute-start | bytes 1769480 | tf_op jit(solution)/shard_map/ppermute | solution.py:33
  231.9 30.4 %collective-permute-start.28 = (bf16[1536,384]{1,0:T(8,128)(2,1)}, bf16[1536,384]{1,0:T(8,128)(2,1)S(1)}, u32[]{:S(2)}, u32[]{:S(2)}) collective-permute-start(bf16[1536,384]{1,0:T(8,128)(2,1)} %fusion.34), channel_id=1, source_target_pairs={{0,1},{1,0},{2,3},{3,2},{4,5},{5,4},{6,7},{7,6},{8,9},{9,8},{10,11... | collective-permute-start | bytes 3538952 | tf_op jit(solution)/shard_map/ppermute | solution.py:33
  240.0 55.1 %collective-permute-start.29 = (bf16[384,1536]{1,0:T(8,128)(2,1)}, bf16[384,1536]{1,0:T(8,128)(2,1)S(1)}, u32[]{:S(2)}, u32[]{:S(2)}) collective-permute-start(bf16[384,1536]{1,0:T(8,128)(2,1)} %fusion.35), channel_id=1, source_target_pairs={{0,1},{1,0},{2,3},{3,2},{4,5},{5,4},{6,7},{7,6},{8,9},{9,8},{10,11... | collective-permute-start | bytes 3538952 | tf_op jit(solution)/shard_map/ppermute | solution.py:33
  263.2 29.8 %collective-permute-start.30 = (bf16[768,384]{1,0:T(8,128)(2,1)}, bf16[768,384]{1,0:T(8,128)(2,1)}, u32[]{:S(2)}, u32[]{:S(2)}) collective-permute-start(bf16[768,384]{1,0:T(8,128)(2,1)} %fusion.5), channel_id=1, source_target_pairs={{0,4},{4,0},{8,12},{12,8},{16,20},{20,16},{24,28},{28,24},{1,5},{5... | collective-permute-start | bytes 1769480 | tf_op jit(solution)/shard_map/ppermute | solution.py:38
  304.6 32.4 %collective-permute-start.32 = (bf16[384,1536]{1,0:T(8,128)(2,1)}, bf16[384,1536]{1,0:T(8,128)(2,1)}, u32[]{:S(2)}, u32[]{:S(2)}) collective-permute-start(bf16[384,1536]{1,0:T(8,128)(2,1)} %pad_maximum_fusion.2), channel_id=1, source_target_pairs={{0,1},{1,0},{2,3},{3,2},{4,5},{5,4},{6,7},{7,6},{8,9},{9,8},{10,11... | collective-permute-start | bytes 3538952 | tf_op jit(solution)/shard_map/ppermute | solution.py:33
  310.5 26.2 %collective-permute-start.33 = (bf16[192,1536]{1,0:T(8,128)(2,1)}, bf16[192,1536]{1,0:T(8,128)(2,1)S(1)}, u32[]{:S(2)}, u32[]{:S(2)}) collective-permute-start(bf16[192,1536]{1,0:T(8,128)(2,1)} %fusion.6), channel_id=1, source_target_pairs={{0,4},{4,0},{8,12},{12,8},{16,20},{20,16},{24,28},{28,24},{1,5},{5... | collective-permute-start | bytes 1769480 | tf_op jit(solution)/shard_map/ppermute | solution.py:38
  327.0 58.2 %collective-permute-start.38 = (bf16[1536,384]{1,0:T(8,128)(2,1)}, bf16[1536,384]{1,0:T(8,128)(2,1)}, u32[]{:S(2)}, u32[]{:S(2)}) collective-permute-start(bf16[1536,384]{1,0:T(8,128)(2,1)} %fusion.42), channel_id=1, source_target_pairs={{0,1},{1,0},{2,3},{3,2},{4,5},{5,4},{6,7},{7,6},{8,9},{9,8},{10,11... | collective-permute-start | bytes 3538952 | tf_op jit(solution)/shard_map/ppermute | solution.py:33
  327.2 35.2 %collective-permute-start.36 = (bf16[768,384]{1,0:T(8,128)(2,1)S(1)}, bf16[768,384]{1,0:T(8,128)(2,1)}, u32[]{:S(2)}, u32[]{:S(2)}) collective-permute-start(bf16[768,384]{1,0:T(8,128)(2,1)S(1)} %add_convert_fusion.8), channel_id=1, source_target_pairs={{0,16},{4,20},{8,24},{12,28},{16,0},{20,4},{24,8},{28,12},{1,17},{... | collective-permute-start | bytes 1769480 | tf_op jit(solution)/shard_map/ppermute | solution.py:38
  337.0 29.3 %collective-permute-start.35 = (bf16[192,1536]{1,0:T(8,128)(2,1)S(1)}, bf16[192,1536]{1,0:T(8,128)(2,1)}, u32[]{:S(2)}, u32[]{:S(2)}) collective-permute-start(bf16[192,1536]{1,0:T(8,128)(2,1)S(1)} %fusion.1), channel_id=1, source_target_pairs={{0,8},{4,12},{8,0},{12,4},{16,24},{20,28},{24,16},{28,20},{1,9},{5... | collective-permute-start | bytes 1769480 | tf_op jit(solution)/shard_map/ppermute | solution.py:38
  338.2 40.7 %collective-permute-start.39 = (bf16[192,1536]{1,0:T(8,128)(2,1)S(1)}, bf16[192,1536]{1,0:T(8,128)(2,1)}, u32[]{:S(2)}, u32[]{:S(2)}) collective-permute-start(bf16[192,1536]{1,0:T(8,128)(2,1)S(1)} %fusion.7), channel_id=1, source_target_pairs={{0,4},{4,0},{8,12},{12,8},{16,20},{20,16},{24,28},{28,24},{1,5},{5... | collective-permute-start | bytes 1769480 | tf_op jit(solution)/shard_map/ppermute | solution.py:38
  348.1 20.1 %collective-permute-start.37 = (bf16[1024,768]{1,0:T(8,128)(2,1)S(1)}, bf16[1024,768]{1,0:T(8,128)(2,1)S(1)}, u32[]{:S(2)}, u32[]{:S(2)}) collective-permute-start(bf16[1024,768]{1,0:T(8,128)(2,1)S(1)} %get-tuple-element.302.refs_1_), channel_id=1, source_target_pairs={{0,2},{2,0},{1,3},{3,1},{4,6},{6,4},{5,7},{7,5},{8,10},{10,8},{9,1... | collective-permute-start | bytes 4718600 | tf_op jit(solution)/shard_map/ppermute | solution.py:33
  362.4 57.2 %collective-permute-start.43 = (bf16[384,1536]{1,0:T(8,128)(2,1)}, bf16[384,1536]{1,0:T(8,128)(2,1)}, u32[]{:S(2)}, u32[]{:S(2)}) collective-permute-start(bf16[384,1536]{1,0:T(8,128)(2,1)} %fusion.43), channel_id=1, source_target_pairs={{0,1},{1,0},{2,3},{3,2},{4,5},{5,4},{6,7},{7,6},{8,9},{9,8},{10,11... | collective-permute-start | bytes 3538952 | tf_op jit(solution)/shard_map/ppermute | solution.py:33
  368.2 44.2 %collective-permute-start.41 = (bf16[192,1536]{1,0:T(8,128)(2,1)}, bf16[192,1536]{1,0:T(8,128)(2,1)}, u32[]{:S(2)}, u32[]{:S(2)}) collective-permute-start(bf16[192,1536]{1,0:T(8,128)(2,1)} %add_convert_fusion.5), channel_id=1, source_target_pairs={{0,16},{4,20},{8,24},{12,28},{16,0},{20,4},{24,8},{28,12},{1,17},{... | collective-permute-start | bytes 1769480 | tf_op jit(solution)/shard_map/ppermute | solution.py:38
  368.2 157.3 %collective-permute-start.74 = (bf16[768,384]{1,0:T(8,128)(2,1)}, bf16[768,384]{1,0:T(8,128)(2,1)}, u32[]{:S(2)}, u32[]{:S(2)}) collective-permute-start(bf16[768,384]{1,0:T(8,128)(2,1)} %add_convert_fusion.6.refs_2_), channel_id=1, source_target_pairs={{0,4},{4,0},{8,12},{12,8},{16,20},{20,16},{24,28},{28,24},{1,5},{5... | collective-permute-start | bytes 1769480 | tf_op jit(solution)/shard_map/ppermute | solution.py:38
  381.2 35.0 %collective-permute-start.40 = (bf16[192,1536]{1,0:T(8,128)(2,1)}, bf16[192,1536]{1,0:T(8,128)(2,1)}, u32[]{:S(2)}, u32[]{:S(2)}) collective-permute-start(bf16[192,1536]{1,0:T(8,128)(2,1)} %fusion), channel_id=1, source_target_pairs={{0,8},{4,12},{8,0},{12,4},{16,24},{20,28},{24,16},{28,20},{1,9},{5... | collective-permute-start | bytes 1769480 | tf_op jit(solution)/shard_map/ppermute | solution.py:38
  387.7 30.2 %collective-permute-start.44 = (bf16[768,384]{1,0:T(8,128)(2,1)}, bf16[768,384]{1,0:T(8,128)(2,1)}, u32[]{:S(2)}, u32[]{:S(2)}) collective-permute-start(bf16[768,384]{1,0:T(8,128)(2,1)} %get-tuple-element.387), channel_id=1, source_target_pairs={{0,4},{4,0},{8,12},{12,8},{16,20},{20,16},{24,28},{28,24},{1,5},{5... | collective-permute-start | bytes 1769480 | tf_op jit(solution)/shard_map/ppermute | solution.py:38
  413.8 25.1 %collective-permute-start.47 = (bf16[192,1536]{1,0:T(8,128)(2,1)S(1)}, bf16[192,1536]{1,0:T(8,128)(2,1)S(1)}, u32[]{:S(2)}, u32[]{:S(2)}) collective-permute-start(bf16[192,1536]{1,0:T(8,128)(2,1)S(1)} %add_convert_fusion.3.refs_2_), channel_id=1, source_target_pairs={{0,4},{4,0},{8,12},{12,8},{16,20},{20,16},{24,28},{28,24},{1,5},{5... | collective-permute-start | bytes 1769480 | tf_op jit(solution)/shard_map/ppermute | solution.py:38
  421.9 20.9 %collective-permute-start.45 = (bf16[192,1536]{1,0:T(8,128)(2,1)}, bf16[192,1536]{1,0:T(8,128)(2,1)S(1)}, u32[]{:S(2)}, u32[]{:S(2)}) collective-permute-start(bf16[192,1536]{1,0:T(8,128)(2,1)} %get-tuple-element.384), channel_id=1, source_target_pairs={{0,4},{4,0},{8,12},{12,8},{16,20},{20,16},{24,28},{28,24},{1,5},{5... | collective-permute-start | bytes 1769480 | tf_op jit(solution)/shard_map/ppermute | solution.py:38
  422.8 35.4 %collective-permute-start.42 = (bf16[192,1536]{1,0:T(8,128)(2,1)S(1)}, bf16[192,1536]{1,0:T(8,128)(2,1)S(1)}, u32[]{:S(2)}, u32[]{:S(2)}) collective-permute-start(bf16[192,1536]{1,0:T(8,128)(2,1)S(1)} %add_convert_fusion.2), channel_id=1, source_target_pairs={{0,16},{4,20},{8,24},{12,28},{16,0},{20,4},{24,8},{28,12},{1,17},{... | collective-permute-start | bytes 1769480 | tf_op jit(solution)/shard_map/ppermute | solution.py:38
  438.9 25.7 %collective-permute-start.53 = (bf16[384,1152]{1,0:T(8,128)(2,1)}, bf16[384,1152]{1,0:T(8,128)(2,1)}, u32[]{:S(2)}, u32[]{:S(2)}) collective-permute-start(bf16[384,1152]{1,0:T(8,128)(2,1)} %pad_maximum_fusion.3), channel_id=1, source_target_pairs={{0,1},{1,0},{2,3},{3,2},{4,5},{5,4},{6,7},{7,6},{8,9},{9,8},{10,11... | collective-permute-start | bytes 2654216 | tf_op jit(solution)/shard_map/ppermute | solution.py:33
  439.3 34.3 %collective-permute-start.50 = (bf16[384,384]{1,0:T(8,128)(2,1)}, bf16[384,384]{1,0:T(8,128)(2,1)}, u32[]{:S(2)}, u32[]{:S(2)}) collective-permute-start(bf16[384,384]{1,0:T(8,128)(2,1)} %fusion.50), channel_id=1, source_target_pairs={{0,1},{1,0},{2,3},{3,2},{4,5},{5,4},{6,7},{7,6},{8,9},{9,8},{10,11... | collective-permute-start | bytes 884744 | tf_op jit(solution)/shard_map/ppermute | solution.py:33
  442.8 24.8 %collective-permute-start.52 = (bf16[384,384]{1,0:T(8,128)(2,1)}, bf16[384,384]{1,0:T(8,128)(2,1)}, u32[]{:S(2)}, u32[]{:S(2)}) collective-permute-start(bf16[384,384]{1,0:T(8,128)(2,1)} %fusion.11), channel_id=1, source_target_pairs={{0,16},{4,20},{8,24},{12,28},{16,0},{20,4},{24,8},{28,12},{1,17},{... | collective-permute-start | bytes 884744 | tf_op jit(solution)/shard_map/ppermute | solution.py:38
  482.5 24.3 %collective-permute-start.63 = (bf16[96,1152]{1,0:T(8,128)(2,1)S(1)}, bf16[96,1152]{1,0:T(8,128)(2,1)S(1)}, u32[]{:S(2)}, u32[]{:S(2)}) collective-permute-start(bf16[96,1152]{1,0:T(8,128)(2,1)S(1)} %fusion.18), channel_id=1, source_target_pairs={{0,8},{4,12},{8,0},{12,4},{16,24},{20,28},{24,16},{28,20},{1,9},{5... | collective-permute-start | bytes 663560 | tf_op jit(solution)/shard_map/ppermute | solution.py:38
  505.2 25.9 %collective-permute-start.66 = (bf16[1024,384]{1,0:T(8,128)(2,1)}, bf16[1024,384]{1,0:T(8,128)(2,1)}, u32[]{:S(2)}, u32[]{:S(2)}) collective-permute-start(bf16[1024,384]{1,0:T(8,128)(2,1)} %get-tuple-element.382), channel_id=1, source_target_pairs={{1,2},{2,1},{5,6},{6,5},{9,10},{10,9},{13,14},{14,13},{17,18},{18,... | collective-permute-start | bytes 2359304 | tf_op jit(solution)/shard_map/ppermute | solution.py:678
  511.8 49.6 %collective-permute-start.73 = (bf16[192,1536]{1,0:T(8,128)(2,1)S(1)}, bf16[192,1536]{1,0:T(8,128)(2,1)S(1)}, u32[]{:S(2)}, u32[]{:S(2)}) collective-permute-start(bf16[192,1536]{1,0:T(8,128)(2,1)S(1)} %add_convert_fusion.refs_2_), channel_id=1, source_target_pairs={{0,4},{4,0},{8,12},{12,8},{16,20},{20,16},{24,28},{28,24},{1,5},{5... | collective-permute-start | bytes 1769480 | tf_op jit(solution)/shard_map/ppermute | solution.py:38
  512.7 34.2 %collective-permute-start.59 = (bf16[1024,384]{1,0:T(8,128)(2,1)}, bf16[1024,384]{1,0:T(8,128)(2,1)}, u32[]{:S(2)}, u32[]{:S(2)}) collective-permute-start(bf16[1024,384]{1,0:T(8,128)(2,1)} %get-tuple-element.354), channel_id=1, source_target_pairs={{0,1},{3,2},{4,5},{7,6},{8,9},{11,10},{12,13},{15,14},{16,17},{19,... | collective-permute-start | bytes 2359304 | tf_op jit(solution)/shard_map/ppermute | solution.py:678
  (178 other events, 1321.7 us)
